TPU v7x, 256 devices: a whole 4x4x8 slice. The times are simulated.
256 devices in a mesh: row: 8 (over y, core), col: 32 (over z, x).
Axes of the slice: x: 4, y: 4, z: 8, core: 2. Of those that a mesh axis runs over, the one named last changes fastest.
Arguments:
- embeddings: bfloat16 [64, 65536], P(None, ('row', 'col')), may hold values from -6 to 6
- latent: float32 [65536], P(('row', 'col')), may hold values from -162 to 162
- list_of: int32 [65536], P(('row', 'col')), may hold values from 0 to 8191, as said below
- rank_of: int32 [65536], P(('row', 'col')), may hold values from 0 to 7, as said below
- probes: float32 [15, 65536], P(None, ('row', 'col')), may hold values from -6 to 6
Outputs:
- solution: float32 [16, 65536], P(None, ('row', 'col'))
- residual: float32 [16, 65536], P(None, ('row', 'col'))
Inputs may be any that keep to these rules, and one draw needn't show every extreme that they name: `list_of`: the 8 members of every list lie in one aligned block of 256 consecutive completions; every list has exactly 8 members. `rank_of`: within each list the places are 0 to 7, each once.
All inputs are finite; a program needn't handle non-finite values.
Results may differ from a plain program's by a relative error of at most 0.008.
Values may be sent and summed in bfloat16 or wider, within the bound.
No kernel may reach another device: no remote copies, remote signals or barrier semaphores. Data moves between devices by JAX's collectives and lax.ppermute only.
A program may use at most 64 MiB of HBM per device.

v0:
```python
import jax
import jax.numpy as jnp
from jax import lax
from jax.sharding import PartitionSpec as P

ITERS = 2
LIST_LEN = 8


RIDGE = 0.01
block_limit = 4096


def chol_solve(gram, right_side):
    factor = jnp.linalg.cholesky(gram)
    order_n = gram.shape[0]
    forward = []
    for i in range(order_n):
        running = right_side[i]
        for j in range(i):
            running = running - factor[i, j] * forward[j]
        forward.append(running / factor[i, i])
    backward = [None] * order_n
    for i in reversed(range(order_n)):
        running = forward[i]
        for j in range(i + 1, order_n):
            running = running - factor[j, i] * backward[j]
        backward[i] = running / factor[i, i]
    return jnp.stack(backward)


def grams(left_blk, right_blk):
    return lax.dot_general(
        left_blk, right_blk, (((1,), (1,)), ((), ())), precision=lax.Precision.HIGHEST
    )


def plackett_luce_local(latent, list_of, rank_of):
    same_list = list_of[:, None] == list_of[None, :]
    highest = jnp.max(jnp.where(same_list, latent[None, :], -jnp.inf), axis=1)
    shifted = jnp.exp(latent - highest)
    gradient = jnp.ones_like(latent)
    curvature = jnp.zeros_like(latent)
    for section_no in range(LIST_LEN):
        active = rank_of >= section_no
        totals = jnp.sum(jnp.where(same_list & active[None, :], shifted[None, :], 0.0), axis=1)
        chance = shifted / totals
        gradient = gradient - jnp.where(active, chance, 0.0)
        curvature = curvature + jnp.where(active, chance * (1.0 - chance), 0.0)
    return (gradient, curvature)


def square_norms(points):
    widened = points.astype(jnp.float32)
    return jnp.sum(widened * widened, axis=0)


def kernel_tile(left_pts, left_sq, right_pts, right_sq):
    inner_prod = lax.dot_general(
        left_pts, right_pts, (((0,), (0,)), ((), ())), preferred_element_type=jnp.float32
    )
    gamma = 2.0 / left_pts.shape[0]
    return jnp.exp(-gamma * (left_sq[:, None] + right_sq[None, :] - 2.0 * inner_prod)).astype(
        jnp.bfloat16
    )


def per_device(embeddings, latent, list_of, rank_of, probes):
    gradient, curvature = plackett_luce_local(latent, list_of, rank_of)
    root_weight = jnp.sqrt(curvature + RIDGE)
    own_sq = square_norms(embeddings)
    residual = jnp.concatenate([gradient[None, :], probes], axis=0)
    solution = jnp.zeros_like(residual)
    direction = residual
    res_gram = lax.psum(grams(residual, residual), ("row", "col"))
    for step_no in range(ITERS):
        final_step = step_no + 1 == ITERS
        scaled = (root_weight[None, :] * direction).astype(jnp.bfloat16)
        initial = jnp.zeros((scaled.shape[0], embeddings.shape[1]), jnp.float32)
        points = lax.all_gather(embeddings, ("row", "col"), axis=1, tiled=True)
        vectors = lax.all_gather(scaled, ("row", "col"), axis=1, tiled=True)
        piece_len = points.shape[1]

        def sub_step(position, carried):
            offset = position * block_limit
            sub_pts = lax.dynamic_slice_in_dim(points, offset, block_limit, 1)
            sub_vec = lax.dynamic_slice_in_dim(vectors, offset, block_limit, 1)
            kernel = kernel_tile(sub_pts, square_norms(sub_pts), embeddings, own_sq)
            return carried + jnp.dot(sub_vec, kernel, preferred_element_type=jnp.float32)

        image = direction + root_weight[None, :] * lax.fori_loop(
            0, piece_len // block_limit, sub_step, initial
        )
        dir_gram = lax.psum(grams(direction, image), ("row", "col"))
        step_coef = chol_solve(dir_gram, res_gram)
        solution = solution + jnp.dot(step_coef.T, direction, precision=lax.Precision.HIGHEST)
        residual = residual - jnp.dot(step_coef.T, image, precision=lax.Precision.HIGHEST)
        if not final_step:
            new_gram = lax.psum(grams(residual, residual), ("row", "col"))
        if not final_step:
            mix_coef = chol_solve(res_gram, new_gram)
            direction = residual + jnp.dot(mix_coef.T, direction, precision=lax.Precision.HIGHEST)
            res_gram = new_gram
    return (solution, residual)


def solution(mesh):
    in_specs = (
        P(None, ("row", "col")),
        P(("row", "col")),
        P(("row", "col")),
        P(("row", "col")),
        P(None, ("row", "col")),
    )
    out_specs = (P(None, ("row", "col")), P(None, ("row", "col")))
    return jax.shard_map(
        per_device, mesh=mesh, in_specs=in_specs, out_specs=out_specs, check_vma=False
    )
```

profile of v0, /device:TPU:1, one launch (start us, length us, event | category | flops | bytes accessed | tf_op | source)
XLA Modules:
  0.0 1668.0 jit_solution(9417256601613358089)
XLA Ops:
  14.7 106.3 %all-gather.4.cloned.1.call-done = bf16[16,65536]{1,0:T(8,128)(2,1)} async-done(((bf16[16,256]{1,0:T(8,128)(2,1)}), bf16[16,65536]{1,0:T(8,128)(2,1)}) %all-gather.4.cloned.1.call-update) | async-done | bytes 2097168 | tf_op jit(solution)/shard_map/all_gather | solution.py:81
  121.0 121.0 %all-gather.6.cloned.1.call-done = bf16[64,65536]{1,0:T(8,128)(2,1)} async-done(((bf16[64,256]{1,0:T(8,128)(2,1)}), bf16[64,65536]{1,0:T(8,128)(2,1)}) %all-gather.6.cloned.1.call-update) | async-done | bytes 8388624 | tf_op jit(solution)/shard_map/all_gather | solution.py:80
  242.0 60.2 %while.28 = (s32[]{:T(128)}, f32[16,256]{1,0:T(8,128)S(1)}, bf16[16,65536]{1,0:T(8,128)(2,1)}, bf16[64,65536]{1,0:T(8,128)(2,1)}, f32[256]{0:T(256)S(1)}, /*inde...) while((s32[]{:T(128)}, f32[16,256]{1,0:T(8,128)S(1)}, ...), condition=%wide.region_13.14_spmd.clone, body=%wide.region_11.13_spmd.clone.sunk | while | flops 173805568 | bytes 1280672 | solution.py:91
  302.4 77.0 %all-reduce = (f32[16,16]{0,1:T(8,128)S(1)}, f32[16,16]{0,1:T(8,128)S(1)}) all-reduce(f32[16,16]{0,1:T(8,128)S(1)} %fusion.146, f32[16,16]{0,1:T(8,128)S(1)} %fusion.27), channel_id=1, replica_groups=mesh['row'=8,'col'=32] {'row','col'}, use_global_device_ids=true, to_apply=%region_9.10 | all-reduce | flops 512 | bytes 4096 | tf_op jit(solution)/shard_map/psum | solution.py:75
  389.2 65.7 %subtract_divide_fusion.14 = (f32[1,16]{0,1:T(8,128)S(1)}, f32[1,16]{0,1:T(8,128)S(1)}, f32[1,16]{0,1:T(8,128)S(1)}, f32[1,16]{0,1:T(8,128)S(1)}) fusion(f32[16,16]{0,1:T(8,128)S(1)} %get-tuple-element.313, f32[]{:T(128)} %bitcast.106, f32[]{:T(128)} %bitcast.105, f32[]{:T(128)} %bitcast.104, f32[]{:T(128)} %bitcast.103, f32[]{:T(128)} %bitcast.102, ...), kind=kLoop, calls=%fused_computation.85 | loop fusion | flops 3136 | bytes 1572 | tf_op jit(solution)/shard_map/div | solution.py:22
  454.9 75.3 %subtract_divide_fusion.2 = (f32[1,16]{0,1:T(8,128)S(1)}, f32[1,16]{0,1:T(8,128)S(1)}, f32[1,16]{0,1:T(8,128)S(1)}, f32[1,16]{0,1:T(8,128)S(1)}, f32[1,16]{0,1:T...) fusion(f32[1,16]{0,1:T(8,128)S(1)} %get-tuple-element.444, ...), kind=kLoop, calls=%fused_computation.73 | loop fusion | flops 5056 | bytes 2212 | tf_op jit(solution)/shard_map/div | solution.py:28
  530.2 22.9 %subtract_divide_fusion.1 = f32[1,16]{0,1:T(8,128)S(1)} fusion(f32[1,16]{0,1:T(8,128)S(1)} %get-tuple-element.441, f32[1,16]{0,1:T(8,128)S(1)} %get-tuple-element.440, f32[1,16]{0,1:T(8,128)S(1)} %get-tuple-element.439, f32[1,16]{0,1:T(8,128)S(1)} %get-tuple-element.438, f32[1,16]{0,1:T(8,128)S(1)} %get-tuple-element.437, ...), kind=kLoop, calls=%fused_computation.72 | loop fusion | flops 1152 | bytes 1232 | tf_op jit(solution)/shard_map/div | solution.py:28
  553.1 29.0 %subtract_divide_fusion = f32[1,16]{0,1:T(8,128)S(1)} fusion(f32[1,16]{0,1:T(8,128)S(1)} %get-tuple-element.441, f32[1,16]{0,1:T(8,128)S(1)} %get-tuple-element.440, f32[1,16]{0,1:T(8,128)S(1)} %get-tuple-element.439, f32[1,16]{0,1:T(8,128)S(1)} %get-tuple-element.438, f32[1,16]{0,1:T(8,128)S(1)} %get-tuple-element.437, f32[1,16]{0,1:T(8,128)S(1)} %get-tuple-element.436, ...), kind=kLoop, calls=%fused_computation.71 | loop fusion | flops 1552 | bytes 1272 | tf_op jit(solution)/shard_map/div | solution.py:28
  591.6 74.4 %subtract_divide_fusion.147 = (f32[16]{0:T(128)S(1)}, f32[16]{0:T(128)S(1)}, f32[16]{0:T(128)S(1)}, f32[16]{0:T(128)S(1)}, f32[16]{0:T(128)S(1)}, /*index=5*/f32...) fusion(f32[16]{0:T(128)S(1)} %get-tuple-element.266, ...), kind=kLoop, calls=%fused_computation.406 | loop fusion | flops 3584 | bytes 2332 | tf_op jit(solution)/shard_map/div | solution.py:22
  666.0 58.2 %subtract_divide_fusion.134 = (f32[16]{0:T(128)S(1)}, f32[16]{0:T(128)S(1)}, f32[16]{0:T(128)S(1)}, f32[16]{0:T(128)S(1)}, f32[16]{0:T(128)S(1)}, /*index=5*/f32...) fusion(f32[16]{0:T(128)S(1)} %get-tuple-element.473, ...), kind=kLoop, calls=%fused_computation.393 | loop fusion | flops 3184 | bytes 2232 | tf_op jit(solution)/shard_map/div | solution.py:28
  724.3 28.1 %divide_bitcast_fusion.2 = (f32[1,16]{1,0:T(1,128)S(1)}, f32[16]{0:T(128)S(1)}, f32[16]{0:T(128)S(1)}) fusion(f32[16]{0:T(128)S(1)} %get-tuple-element.461, f32[16]{0:T(128)S(1)} %get-tuple-element.460, f32[16]{0:T(128)S(1)} %get-tuple-element.459, f32[16]{0:T(128)S(1)} %get-tuple-element.458, f32[16]{0:T(128)S(1)} %get-tuple-element.457, ...), kind=kLoop, calls=%fused_computation.390 | loop fusion | flops 1392 | bytes 1396 | tf_op jit(solution)/shard_map/stack | solution.py:29
  752.9 72.8 %psum.30 = f32[16,16]{1,0:T(8,128)S(1)} all-reduce(f32[16,16]{1,0:T(8,128)S(1)} %fusion.179), channel_id=1, replica_groups=mesh['row'=8,'col'=32] {'row','col'}, use_global_device_ids=true, to_apply=%region_17.19 | all-reduce | flops 256 | bytes 2048 | tf_op jit(solution)/shard_map/psum | solution.py:99
  827.0 74.3 %subtract_divide_fusion.93 = (f32[1,16]{1,0:T(1,128)S(1)}, f32[1,16]{1,0:T(1,128)S(1)}, f32[1,16]{1,0:T(1,128)S(1)}, f32[1,16]{1,0:T(1,128)S(1)}, f32[1,16]{1,0:...) fusion(f32[]{:T(128)} %bitcast.276, ...), kind=kLoop, calls=%fused_computation.350 | loop fusion | flops 3600 | bytes 2400 | tf_op jit(solution)/shard_map/div | solution.py:22
  901.3 73.6 %subtract_divide_fusion.122 = (f32[16]{0:T(128)S(1)}, f32[16]{0:T(128)S(1)}, f32[16]{0:T(128)S(1)}, f32[16]{0:T(128)S(1)}, f32[16]{0:T(128)S(1)}, /*index=5*/f32...) fusion(f32[1,16]{1,0:T(1,128)S(1)} %get-tuple-element.400, ...), kind=kLoop, calls=%fused_computation.380 | loop fusion | flops 3584 | bytes 2332 | tf_op jit(solution)/shard_map/div | solution.py:22
  975.0 57.9 %subtract_divide_fusion.109 = (f32[16]{0:T(128)S(1)}, f32[16]{0:T(128)S(1)}, f32[16]{0:T(128)S(1)}, f32[16]{0:T(128)S(1)}, f32[16]{0:T(128)S(1)}, /*index=5*/f32...) fusion(f32[16]{0:T(128)S(1)} %get-tuple-element.428, ...), kind=kLoop, calls=%fused_computation.367 | loop fusion | flops 3184 | bytes 2232 | tf_op jit(solution)/shard_map/div | solution.py:28
  1032.8 27.6 %divide_bitcast_fusion.1 = (f32[1,16]{1,0:T(1,128)S(1)}, f32[16]{0:T(128)S(1)}, f32[16]{0:T(128)S(1)}) fusion(f32[16]{0:T(128)S(1)} %get-tuple-element.416, f32[16]{0:T(128)S(1)} %get-tuple-element.415, f32[16]{0:T(128)S(1)} %get-tuple-element.414, f32[16]{0:T(128)S(1)} %get-tuple-element.413, f32[16]{0:T(128)S(1)} %get-tuple-element.412, ...), kind=kLoop, calls=%fused_computation.364 | loop fusion | flops 1392 | bytes 1396 | tf_op jit(solution)/shard_map/stack | solution.py:29
  1060.4 57.9 %subtract_divide_fusion.80 = (f32[1,16]{1,0:T(1,128)S(1)}, f32[1,16]{1,0:T(1,128)S(1)}, f32[1,16]{1,0:T(1,128)S(1)}, f32[1,16]{1,0:T(1,128)S(1)}, f32[1,16]{1,0:...) fusion(f32[1,16]{1,0:T(1,128)S(1)} %get-tuple-element.397, ...), kind=kLoop, calls=%fused_computation.337 | loop fusion | flops 3184 | bytes 2232 | tf_op jit(solution)/shard_map/div | solution.py:28
  1119.3 100.0 %all-gather.8.cloned.1.call-done = bf16[16,65536]{1,0:T(8,128)(2,1)} async-done(((bf16[16,256]{1,0:T(8,128)(2,1)}), bf16[16,65536]{1,0:T(8,128)(2,1)}) %all-gather.8.cloned.1.call-update) | async-done | bytes 2097168 | tf_op jit(solution)/shard_map/all_gather | solution.py:81
  1219.3 60.2 %while.29 = (s32[]{:T(128)}, f32[16,256]{1,0:T(8,128)S(1)}, bf16[16,65536]{1,0:T(8,128)(2,1)}, bf16[64,65536]{1,0:T(8,128)(2,1)}, f32[256]{0:T(256)S(1)}, /*inde...) while((s32[]{:T(128)}, f32[16,256]{1,0:T(8,128)S(1)}, ...), condition=%wide.region_20.22_spmd.clone, body=%wide.region_18.21_spmd.clone.sunk | while | flops 173805568 | bytes 1280672 | solution.py:91
  1220.4 2.6 fusion.206
  1228.0 2.6 fusion.206
  1231.7 2.6 fusion.206
  1239.3 2.6 fusion.206
  1243.0 2.6 fusion.206
  1250.5 2.6 fusion.206
  1254.3 2.6 fusion.206
  1279.6 77.0 %psum.31 = f32[16,16]{0,1:T(8,128)S(1)} all-reduce(f32[16,16]{0,1:T(8,128)S(1)} %fusion.28), channel_id=1, replica_groups=mesh['row'=8,'col'=32] {'row','col'}, use_global_device_ids=true, to_apply=%region_21.23 | all-reduce | flops 256 | bytes 2048 | tf_op jit(solution)/shard_map/psum | solution.py:94
  1366.3 75.0 %subtract_divide_fusion.40 = (f32[1,16]{1,0:T(1,128)S(1)}, f32[1,16]{1,0:T(1,128)S(1)}, f32[1,16]{1,0:T(1,128)S(1)}, f32[1,16]{1,0:T(1,128)S(1)}, f32[1,16]{1,0:...) fusion(f32[]{:T(128)} %bitcast.418, ...), kind=kLoop, calls=%fused_computation.296 | loop fusion | flops 3600 | bytes 2400 | tf_op jit(solution)/shard_map/div | solution.py:22
  1441.3 74.3 %subtract_divide_fusion.69 = (f32[16]{0:T(128)S(1)}, f32[16]{0:T(128)S(1)}, f32[16]{0:T(128)S(1)}, f32[16]{0:T(128)S(1)}, f32[16]{0:T(128)S(1)}, /*index=5*/f32[...) fusion(f32[1,16]{1,0:T(1,128)S(1)} %get-tuple-element.342, ...), kind=kLoop, calls=%fused_computation.326 | loop fusion | flops 3584 | bytes 2332 | tf_op jit(solution)/shard_map/div | solution.py:22
  1515.7 58.0 %subtract_divide_fusion.56 = (f32[16]{0:T(128)S(1)}, f32[16]{0:T(128)S(1)}, f32[16]{0:T(128)S(1)}, f32[16]{0:T(128)S(1)}, f32[16]{0:T(128)S(1)}, /*index=5*/f32[...) fusion(f32[16]{0:T(128)S(1)} %get-tuple-element.370, ...), kind=kLoop, calls=%fused_computation.313 | loop fusion | flops 3184 | bytes 2232 | tf_op jit(solution)/shard_map/div | solution.py:28
  1573.7 28.0 %divide_bitcast_fusion = (f32[1,16]{1,0:T(1,128)S(1)}, f32[16]{0:T(128)S(1)}, f32[16]{0:T(128)S(1)}) fusion(f32[16]{0:T(128)S(1)} %get-tuple-element.358, f32[16]{0:T(128)S(1)} %get-tuple-element.357, f32[16]{0:T(128)S(1)} %get-tuple-element.356, f32[16]{0:T(128)S(1)} %get-tuple-element.355, f32[16]{0:T(128)S(1)} %get-tuple-element.354, ...), kind=kLoop, calls=%fused_computation.310 | loop fusion | flops 1392 | bytes 1396 | tf_op jit(solution)/shard_map/stack | solution.py:29
  1601.7 58.0 %subtract_divide_fusion.27 = (f32[1,16]{1,0:T(1,128)S(1)}, f32[1,16]{1,0:T(1,128)S(1)}, f32[1,16]{1,0:T(1,128)S(1)}, f32[1,16]{1,0:T(1,128)S(1)}, f32[1,16]{1,0:...) fusion(f32[1,16]{1,0:T(1,128)S(1)} %get-tuple-element.339, ...), kind=kLoop, calls=%fused_computation.283 | loop fusion | flops 3184 | bytes 2232 | tf_op jit(solution)/shard_map/div | solution.py:28
  (132 shorter events, 139.9 us)
Async XLA Ops:
  7.2 113.8 %all-gather.4.cloned.1.call-start = ((), (), s32[]{:S(2)}) async-start(), calls=%async_computation | async-start | bytes 2105344 | tf_op jit(solution)/shard_map/all_gather | solution.py:81
  12.1 229.9 %all-gather.6.cloned.1.call-start = ((), (), s32[]{:S(2)}) async-start(), calls=%async_computation.1 | async-start | bytes 8421376 | tf_op jit(solution)/shard_map/all_gather | solution.py:80
  12.9 1206.4 %all-gather.8.cloned.1.call-start = ((), (), s32[]{:S(2)}) async-start(), calls=%async_computation.2 | async-start | bytes 2105344 | tf_op jit(solution)/shard_map/all_gather | solution.py:81
  242.0 60.2 %copy-start = (f32[15,256]{1,0:T(8,128)S(1)}, f32[15,256]{1,0:T(8,128)}, u32[]{:S(2)}) copy-start(f32[15,256]{1,0:T(8,128)} %param.14) | copy-start | bytes 46084
Sparse Core Ops, SparseCore 0:
  12.4 108.5 all-gather.3
  124.8 117.1 all-gather.5
  1119.2 99.9 all-gather.7
where the time goes:
time: 1680 us; the launch traced here: 1670 us
  other arithmetic  991 us (59%)
  waiting for transfers between devices  328 us (20%)
  blocking collectives  227 us (14%)
  matrix products  86.1 us (5%)
  local copies, waits for them, and re-layouts  17.8 us (1%)
  between operations  17.5 us (1%)
    div x6, other arithmetic, chol_solve(): forward.append(running / factor[i, i])  437 us
    div x8, other arithmetic, chol_solve(): backward[i] = running / factor[i, i]  417 us
    all_gather x2, waiting for transfers between devices, per_device(): vectors = lax.all_gather(scaled, ('row', 'col'), axis=1, tiled=True)  206 us
    all_gather x1, waiting for transfers between devices, per_device(): points = lax.all_gather(embeddings, ('row', 'col'), axis=1, tiled=True)  121 us
    another operation x3, other arithmetic, chol_solve(): return jnp.stack(backward)  83.6 us
    dot_general x32, matrix products, sub_step(): jnp.dot(sub_vec, kernel, preferred_element_type=jnp.float32)  82.1 us
    psum x1, blocking collectives, per_device(): res_gram = lax.psum(grams(residual, residual), ('row', 'col'))  77 us
    psum x1, blocking collectives, per_device(): dir_gram = lax.psum(grams(direction, image), ('row', 'col'))  77 us
  transfers between devices with their start and end apart: 3, of which 3 were waited for; matrix products, arithmetic and copies ran while one was open for 0% of the time, Pallas kernels for 0%

commit v1 on v0

v1 whole, which is shorter than its diff:
```python
import jax
import jax.numpy as jnp
from jax import lax
from jax.experimental import pallas as pl
from jax.experimental.pallas import tpu as pltpu
from jax.sharding import Mesh
from jax.sharding import PartitionSpec as P

D = 64
SIDES = 16
LIST_LEN = 8
PT = 256
RIDGE = 0.01
GAMMA = 2.0 / D
ALL = ("y", "core", "z", "x")
GROUP_C = ("y", "x")
GROUP_R = ("core", "z")
GRP = 16
SET = GRP * PT
AUG = 80
R_STEP = 2
VMEM = 56 << 20

F32 = jnp.float32
BF16 = jnp.bfloat16


def hdot(a, b, dims):
    return lax.dot_general(
        a, b, (dims, ((), ())), precision=lax.Precision.HIGHEST, preferred_element_type=F32
    )


def split3(v):
    hi = v.astype(BF16).astype(F32)
    mid = (v - hi).astype(BF16).astype(F32)
    lo = (v - hi - mid).astype(BF16).astype(F32)
    return hi, mid, lo


def spd_solve(gram, right):
    n = gram.shape[0]
    lanes = lax.broadcasted_iota(jnp.int32, (n, n), 1)
    rows = lax.broadcasted_iota(jnp.int32, (n, n), 0)
    a, b = 0.5 * (gram + gram.T), right
    for k in range(n):
        pivot = a[k : k + 1, k : k + 1]
        column = a[:, k : k + 1]
        factor = jnp.where(rows[:, :1] == k, 0.0, column / pivot)
        a_row, b_row = a[k : k + 1, :], b[k : k + 1, :]
        a = a - factor * a_row
        b = b - factor * b_row
    diagonal = jnp.sum(jnp.where(lanes == rows, a, 0.0), axis=1, keepdims=True)
    return b / diagonal


def prepare(emb, latent, list_of, rank_of, probes, msg_c, msg_r, resid, weight):
    row = jnp.concatenate(
        [
            latent[...],
            list_of[...].astype(F32),
            rank_of[...].astype(F32),
            jnp.zeros((5, PT), F32),
        ],
        axis=0,
    )
    col = row.T
    same = col[:, 1:2] == row[1:2, :]
    highest = jnp.max(jnp.where(same, col[:, 0:1], -jnp.inf), axis=0, keepdims=True)
    shifted = jnp.exp(row[0:1, :] - highest)
    shifted_col = jnp.broadcast_to(shifted, (8, PT)).T[:, 0:1]
    gradient = jnp.ones((1, PT), F32)
    curvature = jnp.zeros((1, PT), F32)
    for k in range(LIST_LEN):
        held = jnp.where(col[:, 2:3] >= k, shifted_col, 0.0)
        totals = jnp.sum(jnp.where(same, held, 0.0), axis=0, keepdims=True)
        chance = shifted / totals
        active = row[2:3, :] >= k
        gradient = gradient - jnp.where(active, chance, 0.0)
        curvature = curvature + jnp.where(active, chance * (1.0 - chance), 0.0)
    w = jnp.sqrt(curvature + RIDGE)
    r0 = jnp.concatenate([gradient, probes[...]], axis=0)
    resid[...] = r0
    weight[...] = w
    points = emb[...].astype(F32)
    sq = -GAMMA * jnp.sum(points * points, axis=0, keepdims=True)
    parts = jnp.concatenate(split3(sq), axis=0)
    ones = jnp.ones((3, PT), F32)
    zeros = jnp.zeros((AUG - D - 6, PT), F32)
    to_c = jnp.concatenate([points, ones, parts, zeros, w * r0], axis=0).astype(BF16)
    to_r = jnp.concatenate([points * (2.0 * GAMMA), parts, ones, zeros], axis=0).astype(BF16)
    for g in range(GRP):
        msg_c[g] = to_c
        msg_r[g] = to_r


def first_apply(c_ref, r_ref, out, tile, left, vec):
    @pl.when(pl.program_id(0) == 0)
    def _():
        for g in range(GRP):
            left[g * PT : (g + 1) * PT, :] = c_ref[g, :AUG, :].T
            vec[:, g * PT : (g + 1) * PT] = c_ref[g, AUG:, :]

    right = jnp.concatenate([r_ref[i] for i in range(R_STEP)], axis=1)
    step = 512
    total = jnp.zeros((SIDES, R_STEP * PT), F32)
    for j in range(SET // step):
        at = slice(j * step, (j + 1) * step)
        exponent = jnp.dot(left[at, :], right, preferred_element_type=F32)
        kernel = jnp.exp(exponent).astype(BF16)
        tile[at, :] = kernel
        total += jnp.dot(vec[:, at], kernel, preferred_element_type=F32)
    for i in range(R_STEP):
        out[i] = total[:, i * PT : (i + 1) * PT]


def moments(all_ref, out):
    total = jnp.zeros((2 * SIDES, 2 * SIDES), F32)
    for g in range(GRP):
        block = all_ref[g, : 2 * SIDES, :]
        total += hdot(block, block, ((1,), (1,)))
    rr = total[:SIDES, :SIDES]
    ri = total[:SIDES, SIDES:]
    ii = total[SIDES:, SIDES:]
    packed = jnp.concatenate(
        [rr[:8], rr[8:], ri[:8], ri[8:], ii[:8], ii[8:], jnp.zeros((8, 32), F32)], axis=1
    )
    for g in range(GRP):
        out[g] = packed


def unpack(total, n):
    return jnp.concatenate(
        [total[:, 32 * n : 32 * n + 16], total[:, 32 * n + 16 : 32 * n + 32]], axis=0
    )


def second_apply(
    mom, all_ref, res_ref, img_ref, tile, out, sol1, res1, dir1, gram1, vec
):
    @pl.when(pl.program_id(0) == 0)
    def _():
        total = jnp.sum(mom[...], axis=0)
        rr, ri, ii = unpack(total, 0), unpack(total, 1), unpack(total, 2)
        step = spd_solve(ri, rr)
        cross = hdot(step, ri, ((0,), (1,)))
        new = rr - cross - cross.T + hdot(step, hdot(ii, step, ((1,), (0,))), ((0,), (0,)))
        mix = spd_solve(rr, new)
        gram1[...] = new

        def advance(r0, i0):
            r1 = r0 - hdot(step, i0, ((0,), (0,)))
            return r1, r1 + hdot(mix, r0, ((0,), (0,)))

        r1, d1 = advance(res_ref[...], img_ref[...])
        sol1[...] = hdot(step, res_ref[...], ((0,), (0,)))
        res1[...] = r1
        dir1[...] = d1
        for g in range(GRP):
            _, d1 = advance(all_ref[g, :SIDES, :], all_ref[g, SIDES : 2 * SIDES, :])
            w = all_ref[g, 2 * SIDES : 2 * SIDES + 1, :]
            vec[:, g * PT : (g + 1) * PT] = (w * d1).astype(BF16)

    total = jnp.dot(vec[...], tile[...], preferred_element_type=F32)
    for i in range(R_STEP):
        out[i] = total[:, i * PT : (i + 1) * PT]


def first_image(parts, base, w, out, image):
    total = parts[0]
    for g in range(1, GRP):
        total = total + parts[g]
    img = base[...] + w[...] * total
    image[...] = img
    message = jnp.concatenate([base[...], img, jnp.broadcast_to(w[...], (8, PT))], axis=0)
    for g in range(GRP):
        out[g] = message


def second_image(parts, base, w, out, image):
    total = parts[0]
    for g in range(1, GRP):
        total = total + parts[g]
    img = base[...] + w[...] * total
    image[...] = img
    gram = hdot(base[...], img, ((1,), (1,)))
    top = jnp.concatenate([gram[i : i + 1] for i in range(8)], axis=1)
    bottom = jnp.concatenate([gram[i : i + 1] for i in range(8, 16)], axis=1)
    packed = jnp.concatenate([top, bottom], axis=0)
    out[...] = jnp.broadcast_to(packed[None], out.shape)


def finish(grams, gram1, sol1, res1, dir1, img1, sol, res):
    total = jnp.sum(grams[...], axis=0)
    gram = jnp.concatenate(
        [total[i // 8 : i // 8 + 1, 16 * (i % 8) : 16 * (i % 8) + 16] for i in range(16)], axis=0
    )
    step = spd_solve(gram, gram1[...])
    sol[...] = sol1[...] + hdot(step, dir1[...], ((0,), (0,)))
    res[...] = res1[...] - hdot(step, img1[...], ((0,), (0,)))


def shape(*dims, dtype=F32):
    return jax.ShapeDtypeStruct(dims, dtype)


def call(body, out, **more):
    return pl.pallas_call(
        body,
        out_shape=out,
        compiler_params=pltpu.CompilerParams(vmem_limit_bytes=VMEM),
        **more,
    )


def whole(*dims):
    return pl.BlockSpec(dims, lambda i: (0,) * len(dims))


def per_device(embeddings, latent, list_of, rank_of, probes):
    msg_c, msg_r, res0, w = call(
        prepare,
        (
            shape(GRP, AUG + SIDES, PT, dtype=BF16),
            shape(GRP, AUG, PT, dtype=BF16),
            shape(SIDES, PT),
            shape(1, PT),
        ),
        name="prepare",
    )(embeddings, latent[None, :], list_of[None, :], rank_of[None, :], probes)
    all_c = lax.all_to_all(msg_c, GROUP_C, 0, 0, tiled=True)
    all_r = lax.all_to_all(msg_r, GROUP_R, 0, 0, tiled=True)

    n_steps = GRP // R_STEP
    part_spec = pl.BlockSpec((R_STEP, SIDES, PT), lambda i: (i, 0, 0))
    tile_spec = pl.BlockSpec((None, SET, R_STEP * PT), lambda i: (i, 0, 0))
    part, tiles = call(
        first_apply,
        (shape(GRP, SIDES, PT), shape(n_steps, SET, R_STEP * PT, dtype=BF16)),
        grid=(n_steps,),
        in_specs=[
            whole(GRP, AUG + SIDES, PT),
            pl.BlockSpec((R_STEP, AUG, PT), lambda i: (i, 0, 0)),
        ],
        out_specs=(part_spec, tile_spec),
        scratch_shapes=[pltpu.VMEM((SET, AUG), BF16), pltpu.VMEM((SIDES, SET), BF16)],
        name="first_apply",
    )(all_c, all_r)
    part = lax.all_to_all(part, GROUP_R, 0, 0, tiled=True)

    message, img0 = call(
        first_image, (shape(GRP, 2 * SIDES + 8, PT), shape(SIDES, PT)), name="first_image"
    )(part, res0, w)
    everyone = lax.all_to_all(message, GROUP_C, 0, 0, tiled=True)
    mom = call(moments, shape(GRP, 8, 128), name="moments")(everyone)
    mom = lax.all_to_all(mom, GROUP_R, 0, 0, tiled=True)

    part, sol1, res1, dir1, gram1 = call(
        second_apply,
        (
            shape(GRP, SIDES, PT),
            shape(SIDES, PT),
            shape(SIDES, PT),
            shape(SIDES, PT),
            shape(SIDES, SIDES),
        ),
        grid=(n_steps,),
        in_specs=[
            whole(GRP, 8, 128),
            whole(GRP, 2 * SIDES + 8, PT),
            whole(SIDES, PT),
            whole(SIDES, PT),
            tile_spec,
        ],
        out_specs=(
            part_spec,
            whole(SIDES, PT),
            whole(SIDES, PT),
            whole(SIDES, PT),
            whole(SIDES, SIDES),
        ),
        scratch_shapes=[pltpu.VMEM((SIDES, SET), BF16)],
        name="second_apply",
    )(mom, everyone, res0, img0, tiles)
    part = lax.all_to_all(part, GROUP_R, 0, 0, tiled=True)

    grams, img1 = call(
        second_image, (shape(256, 2, 128), shape(SIDES, PT)), name="second_image"
    )(part, dir1, w)
    grams = lax.all_to_all(grams, ALL, 0, 0, tiled=True)
    return call(finish, (shape(SIDES, PT), shape(SIDES, PT)), name="finish")(
        grams, gram1, sol1, res1, dir1, img1
    )


def solution(mesh):
    grid = Mesh(mesh.devices.reshape(4, 2, 8, 4), ALL)
    in_specs = (P(None, ALL), P(ALL), P(ALL), P(ALL), P(None, ALL))
    return jax.shard_map(
        per_device,
        mesh=grid,
        in_specs=in_specs,
        out_specs=(P(None, ALL), P(None, ALL)),
        check_vma=False,
    )
```

time: 1680 us -> 185 us (0.11)
  other arithmetic: 991 us -> 0 us
  waiting for transfers between devices: 328 us -> 0 us
  blocking collectives: 227 us -> 132 us
  matrix products: 86.1 us -> 0 us
  Pallas kernels: 0 us -> 51.4 us
  local copies, waits for them, and re-layouts: 17.8 us -> 0 us
  between operations: 17.5 us -> 0.64 us
    div x16 -> x0, other arithmetic: 855 us -> none  [the longest x6 437 us: chol_solve(): forward.append(running / factor[i, i])]
    all_gather x3 -> x0, waiting for transfers between devices: 327 us -> none  [the longest x2 206 us: per_device(): vectors = lax.all_gather(scaled, ('row', 'col'), axis=1, tiled=True)]
    psum x3 -> x0, blocking collectives: 227 us -> none  [the longest x1 77 us: per_device(): res_gram = lax.psum(grams(residual, residual), ('row', 'col'))]
    all_to_all x0 -> x7, blocking collectives: none -> 132 us  [the longest x1 29.1 us: per_device(): all_r = lax.all_to_all(msg_r, GROUP_R, 0, 0, tiled=True)]
    another operation x12 -> x0, other arithmetic: 90 us -> none  [the longest x3 83.6 us: chol_solve(): return jnp.stack(backward)]
    dot_general x41 -> x0, matrix products: 86.1 us -> none  [the longest x32 82.1 us: sub_step(): jnp.dot(sub_vec, kernel, preferred_element_type=jnp.float32)]
    pallas_call x0 -> x7, Pallas kernels: none -> 51.4 us  [the longest x1 21.3 us: per_device(): call(first_apply, (shape(GRP, SIDES, PT), shape(n_steps, SET, R_STEP * PT...]
    reduce_sum x34 -> x0, other arithmetic: 40.1 us -> none  [the longest x33 38.9 us: square_norms(): return jnp.sum(widened * widened, axis=0)]
  transfers between devices with their start and end apart: 3 -> 0, of which waited for: 3 -> 0; matrix products, arithmetic and copies ran while one was open for 0% -> 0% of each run, Pallas kernels for 0% -> 0%
where the time goes in v1:
time: 185 us; the launch traced here: 184 us
  blocking collectives  132 us (71%)
  Pallas kernels  51.4 us (28%)
    all_to_all x1, blocking collectives, per_device(): all_r = lax.all_to_all(msg_r, GROUP_R, 0, 0, tiled=True)  29.1 us
    all_to_all x2, blocking collectives, per_device(): part = lax.all_to_all(part, GROUP_R, 0, 0, tiled=True)  29.1 us
    all_to_all x1, blocking collectives, per_device(): grams = lax.all_to_all(grams, ALL, 0, 0, tiled=True)  22.5 us
    pallas_call x1, Pallas kernels, per_device(): call(first_apply, (shape(GRP, SIDES, PT), shape(n_steps, SET, R_STEP * PT...  21.3 us
    all_to_all x1, blocking collectives, per_device(): all_c = lax.all_to_all(msg_c, GROUP_C, 0, 0, tiled=True)  21.2 us
    pallas_call x1, Pallas kernels, per_device(): call(second_apply, (shape(GRP, SIDES, PT), shape(SIDES, PT), shape(SIDES,...  17.4 us
    all_to_all x1, blocking collectives, per_device(): everyone = lax.all_to_all(message, GROUP_C, 0, 0, tiled=True)  15.8 us
    all_to_all x1, blocking collectives, per_device(): mom = lax.all_to_all(mom, GROUP_R, 0, 0, tiled=True)  14.4 us

profile of v1, /device:TPU:1, one launch (start us, length us, event | category | flops | bytes accessed | tf_op | source)
XLA Modules:
  0.0 184.1 jit_solution(12577941019787909986)
XLA Ops:
  0.6 2.8 %prepare.1 = (bf16[16,96,256]{2,1,0:T(8,128)(2,1)}, bf16[16,80,256]{2,1,0:T(8,128)(2,1)}, f32[16,256]{1,0:T(8,128)}, f32[1,256]{1,0:T(1,128)}) custom-call(bf16[64,256]{1,0:T(8,128)(2,1)} %emb.1, f32[1,256]{1,0:T(1,128)} %bitcast.3, s32[1,256]{1,0:T(1,128)} %bitcast.4, s32[1,256]{1,0:T(1,128)} %bitcast.5, f32[15,256]{1,0:T(8,128)} %probes.1), custom_call_target="tpu_custom_call" | custom-call | tf_op jit(solution)/shard_map/prepare/pallas_call | solution.py:221
  3.4 21.2 %all_to_all.35.c_ref = bf16[16,96,256]{2,1,0:T(8,128)(2,1)} all-to-all(bf16[16,96,256]{2,1,0:T(8,128)(2,1)} %get-tuple-element.17), channel_id=1, replica_groups=mesh['y'=4,'core'=2,'z'=8,'x'=4] {'y','x'}, dimensions={0} | all-to-all | bytes 1572864 | tf_op jit(solution)/shard_map/all_to_all | solution.py:231
  24.6 29.1 %all_to_all.36.r_ref = bf16[16,80,256]{2,1,0:T(8,128)(2,1)} all-to-all(bf16[16,80,256]{2,1,0:T(8,128)(2,1)} %get-tuple-element.18), channel_id=1, replica_groups=mesh['y'=4,'core'=2,'z'=8,'x'=4] {'core','z'}, dimensions={0} | all-to-all | bytes 1310720 | tf_op jit(solution)/shard_map/all_to_all | solution.py:232
  53.8 21.3 %first_apply.1 = (f32[16,16,256]{2,1,0:T(8,128)}, bf16[8,4096,512]{2,1,0:T(8,128)(2,1)}) custom-call(bf16[16,96,256]{2,1,0:T(8,128)(2,1)} %all_to_all.35.c_ref, bf16[16,80,256]{2,1,0:T(8,128)(2,1)} %all_to_all.36.r_ref), custom_call_target="tpu_custom_call" | custom-call | tf_op jit(solution)/shard_map/first_apply/pallas_call | solution.py:237
  75.1 14.8 %all_to_all.37.parts = f32[16,16,256]{2,1,0:T(8,128)} all-to-all(f32[16,16,256]{2,1,0:T(8,128)} %get-tuple-element.19), channel_id=1, replica_groups=mesh['y'=4,'core'=2,'z'=8,'x'=4] {'core','z'}, dimensions={0} | all-to-all | bytes 524288 | tf_op jit(solution)/shard_map/all_to_all | solution.py:249
  89.9 1.9 %first_image.1 = (f32[16,40,256]{2,1,0:T(8,128)}, f32[16,256]{1,0:T(8,128)}) custom-call(f32[16,16,256]{2,1,0:T(8,128)} %all_to_all.37.parts, f32[16,256]{1,0:T(8,128)} %get-tuple-element.20.base.res_ref, f32[1,256]{1,0:T(1,128)} %get-tuple-element.21.w), custom_call_target="tpu_custom_call" | custom-call | tf_op jit(solution)/shard_map/first_image/pallas_call | solution.py:251
  91.8 15.8 %all_to_all.38.all_ref = f32[16,40,256]{2,1,0:T(8,128)} all-to-all(f32[16,40,256]{2,1,0:T(8,128)} %get-tuple-element.22), channel_id=1, replica_groups=mesh['y'=4,'core'=2,'z'=8,'x'=4] {'y','x'}, dimensions={0} | all-to-all | bytes 1310720 | tf_op jit(solution)/shard_map/all_to_all | solution.py:254
  107.5 2.3 %moments.1 = f32[16,8,128]{2,1,0:T(8,128)} custom-call(f32[16,40,256]{2,1,0:T(8,128)} %all_to_all.38.all_ref), custom_call_target="tpu_custom_call" | custom-call | tf_op jit(solution)/shard_map/moments/pallas_call | solution.py:255
  109.9 14.4 %all_to_all.39.mom = f32[16,8,128]{2,1,0:T(8,128)} all-to-all(f32[16,8,128]{2,1,0:T(8,128)} %moments.1), channel_id=1, replica_groups=mesh['y'=4,'core'=2,'z'=8,'x'=4] {'core','z'}, dimensions={0} | all-to-all | bytes 131072 | tf_op jit(solution)/shard_map/all_to_all | solution.py:256
  124.2 17.4 %second_apply.1 = (f32[16,16,256]{2,1,0:T(8,128)}, f32[16,256]{1,0:T(8,128)}, f32[16,256]{1,0:T(8,128)}, f32[16,256]{1,0:T(8,128)}, f32[16,16]{1,0:T(8,128)}) custom-call(f32[16,8,128]{2,1,0:T(8,128)} %all_to_all.39.mom, f32[16,40,256]{2,1,0:T(8,128)} %all_to_all.38.all_ref, f32[16,256]{1,0:T(8,128)} %get-tuple-element.20.base.res_ref, ...), custom_call_target="tpu_custom_call" | custom-call | tf_op jit(solution)/shard_map/second_apply/pallas_call | solution.py:258
  141.6 14.3 %all_to_all.40.parts = f32[16,16,256]{2,1,0:T(8,128)} all-to-all(f32[16,16,256]{2,1,0:T(8,128)} %get-tuple-element.25), channel_id=1, replica_groups=mesh['y'=4,'core'=2,'z'=8,'x'=4] {'core','z'}, dimensions={0} | all-to-all | bytes 524288 | tf_op jit(solution)/shard_map/all_to_all | solution.py:285
  155.9 2.0 %second_image.1 = (f32[256,2,128]{2,1,0:T(2,128)}, f32[16,256]{1,0:T(8,128)}) custom-call(f32[16,16,256]{2,1,0:T(8,128)} %all_to_all.40.parts, f32[16,256]{1,0:T(8,128)} %get-tuple-element.26.base.dir1, f32[1,256]{1,0:T(1,128)} %get-tuple-element.21.w), custom_call_target="tpu_custom_call" | custom-call | tf_op jit(solution)/shard_map/second_image/pallas_call | solution.py:287
  157.9 22.5 %all_to_all.41.grams = f32[256,2,128]{2,1,0:T(2,128)} all-to-all(f32[256,2,128]{2,1,0:T(2,128)} %get-tuple-element.27), channel_id=1, replica_groups=mesh['y'=4,'core'=2,'z'=8,'x'=4] {'y','core','z','x'}, dimensions={0} | all-to-all | bytes 524288 | tf_op jit(solution)/shard_map/all_to_all | solution.py:290
  180.4 3.6 %finish.1 = (f32[16,256]{1,0:T(8,128)}, f32[16,256]{1,0:T(8,128)}) custom-call(f32[256,2,128]{2,1,0:T(2,128)} %all_to_all.41.grams, f32[16,16]{1,0:T(8,128)} %get-tuple-element.28.gram1, f32[16,256]{1,0:T(8,128)} %get-tuple-element.29.sol1, f32[16,256]{1,0:T(8,128)} %get-tuple-element.30.res1, f32[16,256]{1,0:T(8,128)} %get-tuple-element.26.base.dir1, ...), custom_call_target="tpu_custom_call" | custom-call | tf_op jit(solution)/shard_map/finish/pallas_call | solution.py:291

commit v2 on v1

v2 whole, which is shorter than its diff:
```python
import jax
import jax.numpy as jnp
from jax import lax
from jax.experimental import pallas as pl
from jax.experimental.pallas import tpu as pltpu
from jax.sharding import Mesh
from jax.sharding import PartitionSpec as P

D = 64
SIDES = 16
LIST_LEN = 8
PT = 256
RIDGE = 0.01
GAMMA = 2.0 / D
ALL = ("y", "core", "z", "x")
GROUP_C = ("y", "x")
GROUP_R = ("core", "z")
GRP = 16
DEPTH = 8
COLS = 2 * GRP * PT
ROWS = DEPTH * PT
AUG = 80
PIECES = 8
PIECE = COLS // PIECES

F32 = jnp.float32
BF16 = jnp.bfloat16


def hdot(a, b, dims):
    return lax.dot_general(
        a, b, (dims, ((), ())), precision=lax.Precision.HIGHEST, preferred_element_type=F32
    )


def split3(v):
    hi = v.astype(BF16).astype(F32)
    mid = (v - hi).astype(BF16).astype(F32)
    lo = (v - hi - mid).astype(BF16).astype(F32)
    return hi, mid, lo


def spd_solve(gram, right):
    n = gram.shape[0]
    lanes = lax.broadcasted_iota(jnp.int32, (n, n), 1)
    rows = lax.broadcasted_iota(jnp.int32, (n, n), 0)
    a, b = 0.5 * (gram + gram.T), right
    for k in range(n):
        pivot = a[k : k + 1, k : k + 1]
        column = a[:, k : k + 1]
        factor = jnp.where(rows[:, :1] == k, 0.0, column / pivot)
        a_row, b_row = a[k : k + 1, :], b[k : k + 1, :]
        a = a - factor * a_row
        b = b - factor * b_row
    diagonal = jnp.sum(jnp.where(lanes == rows, a, 0.0), axis=1, keepdims=True)
    return b / diagonal


def prepare(emb, latent, list_of, rank_of, probes, msg_c, msg_r, resid, weight):
    row = jnp.concatenate(
        [
            latent[...],
            list_of[...].astype(F32),
            rank_of[...].astype(F32),
            jnp.zeros((5, PT), F32),
        ],
        axis=0,
    )
    col = row.T
    same = col[:, 1:2] == row[1:2, :]
    highest = jnp.max(jnp.where(same, col[:, 0:1], -jnp.inf), axis=0, keepdims=True)
    shifted = jnp.exp(row[0:1, :] - highest)
    shifted_col = jnp.broadcast_to(shifted, (8, PT)).T[:, 0:1]
    gradient = jnp.ones((1, PT), F32)
    curvature = jnp.zeros((1, PT), F32)
    for k in range(LIST_LEN):
        held = jnp.where(col[:, 2:3] >= k, shifted_col, 0.0)
        totals = jnp.sum(jnp.where(same, held, 0.0), axis=0, keepdims=True)
        chance = shifted / totals
        active = row[2:3, :] >= k
        gradient = gradient - jnp.where(active, chance, 0.0)
        curvature = curvature + jnp.where(active, chance * (1.0 - chance), 0.0)
    w = jnp.sqrt(curvature + RIDGE)
    r0 = jnp.concatenate([gradient, probes[...]], axis=0)
    resid[...] = r0
    weight[...] = w
    scaled = w * r0
    high = scaled.astype(BF16)
    low = (scaled - high.astype(F32)).astype(BF16)
    for g in range(GRP):
        msg_c[g, :D, :] = emb[...]
        msg_c[g, D : D + SIDES, :] = high
        msg_c[g, D + SIDES :, :] = low
    for g in range(DEPTH):
        msg_r[g] = emb[...]


def norm_rows(points):
    sq = -GAMMA * jnp.sum(points * points, axis=0, keepdims=True)
    return jnp.concatenate(split3(sq), axis=0)


def first_apply(own, other, r_ref, out, *more):
    tile, (left, vec) = more[:PIECES], more[PIECES:]
    ones = jnp.ones((3, PT), F32)
    zeros = jnp.zeros((AUG - D - 6, PT), F32)
    for half, ref in enumerate((own, other)):
        for g in range(GRP):
            at = slice((half * GRP + g) * PT, (half * GRP + g + 1) * PT)
            points = ref[g, :D, :].astype(F32)
            rows = jnp.concatenate([points, ones, norm_rows(points), zeros], axis=0)
            left[at, :] = rows.astype(BF16).T
            vec[:, at] = ref[g, D : D + SIDES, :]
    columns = []
    for g in range(DEPTH):
        points = r_ref[g].astype(F32)
        rows = [points * (2.0 * GAMMA), norm_rows(points), ones, zeros]
        columns.append(jnp.concatenate(rows, axis=0).astype(BF16))
    right = jnp.concatenate(columns, axis=1)
    step = 256
    total = jnp.zeros((SIDES, ROWS), F32)
    for j in range(COLS // step):
        at = slice(j * step, (j + 1) * step)
        exponent = jnp.dot(left[at, :], right, preferred_element_type=F32)
        kernel = jnp.exp(exponent).astype(BF16)
        tile[j * step // PIECE][pl.ds(j * step % PIECE, step), :] = kernel
        total += jnp.dot(vec[:, at], kernel, preferred_element_type=F32)
    for g in range(DEPTH):
        out[g] = total[:, g * PT : (g + 1) * PT]


def unpack(total, n):
    return jnp.concatenate(
        [total[:, 32 * n : 32 * n + 16], total[:, 32 * n + 16 : 32 * n + 32]], axis=0
    )


def first_image(parts, base, w, out, image):
    total = parts[0]
    for g in range(1, DEPTH):
        total = total + parts[g]
    r0 = base[...]
    i0 = r0 + w[...] * total
    image[...] = i0
    both = jnp.concatenate([r0, i0], axis=0)
    gram = hdot(both, both, ((1,), (1,)))
    rr, ri, ii = gram[:SIDES, :SIDES], gram[:SIDES, SIDES:], gram[SIDES:, SIDES:]
    packed = [rr[:8], rr[8:], ri[:8], ri[8:], ii[:8], ii[8:], jnp.zeros((8, 160), F32)]
    message = jnp.concatenate([w[...] * i0, jnp.concatenate(packed, axis=1)], axis=0)
    for g in range(GRP):
        out[g] = message


def gram_sum(own, out):
    total = own[0]
    for g in range(1, GRP):
        total = total + own[g]
    for g in range(GRP):
        out[g] = total


def second_apply(
    mom, own_i, other_i, own_s, other_s, res_ref, img_ref, *more
):
    tile, (out, sol1, res1, dir1, gram1) = more[:PIECES], more[PIECES:]
    total = jnp.sum(mom[...], axis=0)
    rr, ri, ii = unpack(total, 0), unpack(total, 1), unpack(total, 2)
    step = spd_solve(ri, rr)
    cross = hdot(step, ri, ((0,), (1,)))
    new = rr - cross - cross.T + hdot(step, hdot(ii, step, ((1,), (0,))), ((0,), (0,)))
    mix = spd_solve(rr, new)
    gram1[...] = new
    r0, i0 = res_ref[...], img_ref[...]
    sol1[...] = hdot(step, r0, ((0,), (0,)))
    r1 = r0 - hdot(step, i0, ((0,), (0,)))
    res1[...] = r1
    dir1[...] = r1 + hdot(mix, r0, ((0,), (0,)))
    rows = lax.broadcasted_iota(jnp.int32, (SIDES, SIDES), 0)
    lanes = lax.broadcasted_iota(jnp.int32, (SIDES, SIDES), 1)
    coef = jnp.concatenate([jnp.where(rows == lanes, 1.0, 0.0) + mix, -step], axis=0)
    vec = []
    for i_ref, s_ref in ((own_i, own_s), (other_i, other_s)):
        for g in range(GRP):
            wr = s_ref[g, :SIDES, :].astype(F32) + s_ref[g, SIDES:, :].astype(F32)
            both = jnp.concatenate([wr, i_ref[g]], axis=0)
            vec.append(hdot(coef, both, ((0,), (0,))).astype(BF16))
    total = jnp.zeros((SIDES, ROWS), F32)
    for j in range(len(vec)):
        kernel = tile[j * PT // PIECE][pl.ds(j * PT % PIECE, PT), :]
        total += jnp.dot(vec[j], kernel, preferred_element_type=F32)
    for g in range(DEPTH):
        out[g] = total[:, g * PT : (g + 1) * PT]


def second_image(parts, base, w, out, image):
    total = parts[0]
    for g in range(1, DEPTH):
        total = total + parts[g]
    img = base[...] + w[...] * total
    image[...] = img
    gram = hdot(base[...], img, ((1,), (1,)))
    top = jnp.concatenate([gram[i : i + 1] for i in range(8)], axis=1)
    bottom = jnp.concatenate([gram[i : i + 1] for i in range(8, 16)], axis=1)
    packed = jnp.concatenate([top, bottom], axis=0)
    out[...] = jnp.broadcast_to(packed[None], out.shape)


def finish(grams, gram1, sol1, res1, dir1, img1, sol, res):
    total = jnp.sum(grams[...], axis=0)
    gram = jnp.concatenate(
        [total[i // 8 : i // 8 + 1, 16 * (i % 8) : 16 * (i % 8) + 16] for i in range(16)], axis=0
    )
    step = spd_solve(gram, gram1[...])
    sol[...] = sol1[...] + hdot(step, dir1[...], ((0,), (0,)))
    res[...] = res1[...] - hdot(step, img1[...], ((0,), (0,)))


def shape(*dims, dtype=F32):
    return jax.ShapeDtypeStruct(dims, dtype)


def call(body, out, vmem=8, **more):
    return pl.pallas_call(
        body,
        out_shape=out,
        compiler_params=pltpu.CompilerParams(vmem_limit_bytes=vmem << 20),
        **more,
    )


def block(*dims, at=None):
    return pl.BlockSpec(dims, lambda i: at or (0,) * len(dims))


def swap_cores(array):
    return lax.ppermute(array, "core", ((0, 1), (1, 0)))


def per_device(embeddings, latent, list_of, rank_of, probes):
    resident = pl.BlockSpec(memory_space=pltpu.VMEM)
    msg_c, msg_r, res0, w = call(
        prepare,
        (
            shape(GRP, D + 2 * SIDES, PT, dtype=BF16),
            shape(DEPTH, D, PT, dtype=BF16),
            shape(SIDES, PT),
            shape(1, PT),
        ),
        name="prepare",
    )(embeddings, latent[None, :], list_of[None, :], rank_of[None, :], probes)
    own_c = lax.all_to_all(msg_c, GROUP_C, 0, 0, tiled=True)
    other_c = swap_cores(own_c)
    all_r = lax.all_to_all(msg_r, "z", 0, 0, tiled=True)

    part, *tile = call(
        first_apply,
        (shape(DEPTH, SIDES, PT), *([pltpu.VMEM((PIECE, ROWS), BF16)] * PIECES)),
        vmem=16,
        out_specs=(pl.BlockSpec((DEPTH, SIDES, PT), lambda: (0, 0, 0)), *([resident] * PIECES)),
        scratch_shapes=[pltpu.VMEM((COLS, AUG), BF16), pltpu.VMEM((SIDES, COLS), BF16)],
        name="first_apply",
    )(own_c, other_c, all_r)
    part = lax.all_to_all(part, "z", 0, 0, tiled=True)

    message, img0 = call(
        first_image, (shape(GRP, SIDES + 8, PT), shape(SIDES, PT)), name="first_image"
    )(part, res0, w)
    own_i = lax.all_to_all(message, GROUP_C, 0, 0, tiled=True)
    other_i = swap_cores(own_i)
    mom = call(
        gram_sum,
        shape(GRP, 8, 128),
        grid=(1,),
        in_specs=[block(GRP, 8, 128, at=(0, 2, 0))],
        out_specs=block(GRP, 8, 128),
        name="gram_sum",
    )(own_i)
    mom = lax.all_to_all(mom, GROUP_R, 0, 0, tiled=True)

    images = block(GRP, SIDES, PT)
    scaled = block(GRP, 2 * SIDES, PT, at=(0, 2, 0))
    own = block(SIDES, PT)
    part, sol1, res1, dir1, gram1 = call(
        second_apply,
        (
            shape(DEPTH, SIDES, PT),
            shape(SIDES, PT),
            shape(SIDES, PT),
            shape(SIDES, PT),
            shape(SIDES, SIDES),
        ),
        vmem=12,
        grid=(1,),
        in_specs=[block(GRP, 8, 128), images, images, scaled, scaled, own, own] + [resident] * PIECES,
        out_specs=(block(DEPTH, SIDES, PT), own, own, own, block(SIDES, SIDES)),
        name="second_apply",
    )(mom, own_i, other_i, own_c, other_c, res0, img0, *tile)
    part = lax.all_to_all(part, "z", 0, 0, tiled=True)

    grams, img1 = call(
        second_image, (shape(256, 2, 128), shape(SIDES, PT)), name="second_image"
    )(part, dir1, w)
    grams = lax.all_to_all(grams, ALL, 0, 0, tiled=True)
    return call(finish, (shape(SIDES, PT), shape(SIDES, PT)), name="finish")(
        grams, gram1, sol1, res1, dir1, img1
    )


def solution(mesh):
    grid = Mesh(mesh.devices.reshape(4, 2, 8, 4), ALL)
    in_specs = (P(None, ALL), P(ALL), P(ALL), P(ALL), P(None, ALL))
    return jax.shard_map(
        per_device,
        mesh=grid,
        in_specs=in_specs,
        out_specs=(P(None, ALL), P(None, ALL)),
        check_vma=False,
    )
```

time: 185 us -> 140 us (0.76)
  blocking collectives: 132 us -> 105 us
  Pallas kernels: 51.4 us -> 25.9 us
  starting transfers between devices: 0 us -> 4.78 us
  local copies, waits for them, and re-layouts: 0 us -> 3.5 us
    pallas_call x5, Pallas kernels: 45.8 us -> 22.9 us  [the longest x1 14.2 us: per_device(): call(first_apply, (shape(DEPTH, SIDES, PT), *[pltpu.VMEM((PIECE, ROWS), B...]
    all_to_all x5, blocking collectives: 95.2 us -> 73.1 us  [the longest x1 20.9 us: per_device(): own_c = lax.all_to_all(msg_c, GROUP_C, 0, 0, tiled=True)]
    ppermute x0 -> x2, starting transfers between devices: none -> 4.78 us  [swap_cores(): return lax.ppermute(array, 'core', ((0, 1), (1, 0)))]
    all_to_all x1, blocking collectives: 14.4 us -> 9.62 us  [per_device(): mom = lax.all_to_all(mom, GROUP_R, 0, 0, tiled=True)]
    unnamed x0 -> x10, local copies, waits for them, and re-layouts: none -> 3.5 us
  transfers between devices with their start and end apart: 0 -> 2, of which waited for: 0 -> 0; matrix products, arithmetic and copies ran while one was open for 0% -> 0% of each run, Pallas kernels for 0% -> 0%
where the time goes in v2:
time: 140 us
  blocking collectives  105 us (75%)
  Pallas kernels  25.9 us (18%)
  starting transfers between devices  4.78 us (3%)
  local copies, waits for them, and re-layouts  3.5 us (2%)
    all_to_all x1, blocking collectives, per_device(): grams = lax.all_to_all(grams, ALL, 0, 0, tiled=True)  22 us
    all_to_all x1, blocking collectives, per_device(): own_c = lax.all_to_all(msg_c, GROUP_C, 0, 0, tiled=True)  20.9 us
    all_to_all x2, blocking collectives, per_device(): part = lax.all_to_all(part, 'z', 0, 0, tiled=True)  20.7 us
    all_to_all x1, blocking collectives, per_device(): all_r = lax.all_to_all(msg_r, 'z', 0, 0, tiled=True)  20.3 us
    pallas_call x1, Pallas kernels, per_device(): call(first_apply, (shape(DEPTH, SIDES, PT), *[pltpu.VMEM((PIECE, ROWS), B...  14.2 us
    all_to_all x1, blocking collectives, per_device(): own_i = lax.all_to_all(message, GROUP_C, 0, 0, tiled=True)  11.1 us
    all_to_all x1, blocking collectives, per_device(): mom = lax.all_to_all(mom, GROUP_R, 0, 0, tiled=True)  9.62 us
    pallas_call x1, Pallas kernels, per_device(): call(second_apply, (shape(DEPTH, SIDES, PT), shape(SIDES, PT), shape(SIDE...  7.59 us
  transfers between devices with their start and end apart: 2, of which 0 were waited for; matrix products, arithmetic and copies ran while one was open for 0% of the time, Pallas kernels for 0%

profile of v2, /device:TPU:1, one launch (start us, length us, event | category | flops | bytes accessed | tf_op | source)
XLA Modules:
  0.0 139.5 jit_solution(3288002399106212339)
XLA Ops:
  0.6 0.0 copy-start
  0.6 0.7 copy-done
  1.4 0.0 copy-start.1
  1.4 0.7 copy-done.1
  2.1 0.0 copy-start.2
  2.1 0.7 copy-done.2
  2.8 0.0 copy-start.3
  2.8 0.7 copy-done.3
  3.5 0.0 copy-start.4
  3.5 0.7 copy-done.4
  4.1 0.9 prepare.1
  5.1 20.9 %all_to_all.35.own.own_s = bf16[16,96,256]{2,1,0:T(8,128)(2,1)S(1)} all-to-all(bf16[16,96,256]{2,1,0:T(8,128)(2,1)S(1)} %get-tuple-element.24), channel_id=1, replica_groups=mesh['y'=4,'core'=2,'z'=8,'x'=4] {'y','x'}, dimensions={0} | all-to-all | bytes 1572864 | tf_op jit(solution)/shard_map/all_to_all | solution.py:251
  26.0 1.8 %collective-permute-start = (bf16[16,96,256]{2,1,0:T(8,128)(2,1)S(1)}, bf16[16,96,256]{2,1,0:T(8,128)(2,1)S(1)}, u32[]{:S(2)}, u32[]{:S(2)}) collective-permute-start(bf16[16,96,256]{2,1,0:T(8,128)(2,1)S(1)} %all_to_all.35.own.own_s), channel_id=1, source_target_pairs={{0,32},{32,0},{1,33},{33,1},{2,34},{34,2},{3,35},{35,3},{4,36},{36... | collective-permute-start | bytes 2359304 | tf_op jit(solution)/shard_map/ppermute | solution.py:236
  27.8 20.3 %all_to_all.36.r_ref = bf16[8,64,256]{2,1,0:T(8,128)(2,1)S(1)} all-to-all(bf16[8,64,256]{2,1,0:T(8,128)(2,1)S(1)} %get-tuple-element.25), channel_id=1, replica_groups=mesh['y'=4,'core'=2,'z'=8,'x'=4] {'z'}, dimensions={0} | all-to-all | bytes 524288 | tf_op jit(solution)/shard_map/all_to_all | solution.py:253
  48.1 0.0 collective-permute-done.other.other_s
  48.1 14.2 %first_apply.1 = (f32[8,16,256]{2,1,0:T(8,128)S(1)}, bf16[1024,2048]{1,0:T(8,128)(2,1)S(1)}, bf16[1024,2048]{1,0:T(8,128)(2,1)S(1)}, bf16[1024,2048]{1,0:T(8,128...) custom-call(bf16[16,96,256]{2,1,0:T(8,128)(2,1)S(1)} %all_to_all.35., ...), custom_call_target="tpu_custom_call" | custom-call | tf_op jit(solution)/shard_map/first_apply/pallas_call | solution.py:255
  62.3 10.6 %all_to_all.37.parts = f32[8,16,256]{2,1,0:T(8,128)S(1)} all-to-all(f32[8,16,256]{2,1,0:T(8,128)S(1)} %get-tuple-element.26), channel_id=1, replica_groups=mesh['y'=4,'core'=2,'z'=8,'x'=4] {'z'}, dimensions={0} | all-to-all | bytes 262144 | tf_op jit(solution)/shard_map/all_to_all | solution.py:263
  72.8 0.2 first_image.1
  73.1 11.1 %all_to_all.38.own.own_i = f32[16,24,256]{2,1,0:T(8,128)S(1)} all-to-all(f32[16,24,256]{2,1,0:T(8,128)S(1)} %get-tuple-element.29), channel_id=1, replica_groups=mesh['y'=4,'core'=2,'z'=8,'x'=4] {'y','x'}, dimensions={0} | all-to-all | bytes 786432 | tf_op jit(solution)/shard_map/all_to_all | solution.py:268
  84.2 3.0 %collective-permute-start.1 = (f32[16,24,256]{2,1,0:T(8,128)S(1)}, f32[16,24,256]{2,1,0:T(8,128)S(1)}, u32[]{:S(2)}, u32[]{:S(2)}) collective-permute-start(f32[16,24,256]{2,1,0:T(8,128)S(1)} %all_to_all.38.own.own_i), channel_id=1, source_target_pairs={{0,32},{32,0},{1,33},{33,1},{2,34},{34,2},{3,35},{35,3},{4,36},{36... | collective-permute-start | bytes 1179656 | tf_op jit(solution)/shard_map/ppermute | solution.py:236
  87.2 9.6 %all_to_all.39.mom = f32[16,8,128]{2,1,0:T(8,128)S(1)} all-to-all(f32[16,8,128]{2,1,0:T(8,128)S(1)} %gram_sum.1), channel_id=1, replica_groups=mesh['y'=4,'core'=2,'z'=8,'x'=4] {'core','z'}, dimensions={0} | all-to-all | bytes 131072 | tf_op jit(solution)/shard_map/all_to_all | solution.py:278
  96.8 0.0 collective-permute-done.1.other_i
  96.8 7.6 %second_apply.1 = (f32[8,16,256]{2,1,0:T(8,128)S(1)}, f32[16,256]{1,0:T(8,128)S(1)}, f32[16,256]{1,0:T(8,128)S(1)}, f32[16,256]{1,0:T(8,128)S(1)}, f32[16,16]{1,0:T(8,128)S(1)}) custom-call(f32[16,8,128]{2,1,0:T(8,128)S(1)} %all_to_all.39.mom, f32[16,24,256]{2,1,0:T(8,128)S(1)} %all_to_all.38.own.own_i, f32[16,24,256]{2,1,0:T(8,128)S(1)} %collective-permute-done.1.other_i, ...), custom_call_target="tpu_custom_call" | custom-call | tf_op jit(solution)/shard_map/second_apply/pallas_call | solution.py:283
  104.4 10.2 %all_to_all.40.parts = f32[8,16,256]{2,1,0:T(8,128)S(1)} all-to-all(f32[8,16,256]{2,1,0:T(8,128)S(1)} %get-tuple-element.39), channel_id=1, replica_groups=mesh['y'=4,'core'=2,'z'=8,'x'=4] {'z'}, dimensions={0} | all-to-all | bytes 262144 | tf_op jit(solution)/shard_map/all_to_all | solution.py:298
  114.6 0.3 second_image.1
  114.9 22.0 %all_to_all.41.grams = f32[256,2,128]{2,1,0:T(2,128)S(1)} all-to-all(f32[256,2,128]{2,1,0:T(2,128)S(1)} %get-tuple-element.41), channel_id=1, replica_groups=mesh['y'=4,'core'=2,'z'=8,'x'=4] {'y','core','z','x'}, dimensions={0} | all-to-all | bytes 524288 | tf_op jit(solution)/shard_map/all_to_all | solution.py:303
  136.9 2.6 %finish.1 = (f32[16,256]{1,0:T(8,128)}, f32[16,256]{1,0:T(8,128)}) custom-call(f32[256,2,128]{2,1,0:T(2,128)S(1)} %all_to_all.41.grams, f32[16,16]{1,0:T(8,128)S(1)} %get-tuple-element.42.gram1, f32[16,256]{1,0:T(8,128)S(1)} %get-tuple-element.43.sol1, f32[16,256]{1,0:T(8,128)S(1)} %get-tuple-element.44.res1, f32[16,256]{1,0:T(8,128)S(1)} %get-tuple-element.40.base.dir1, ...), custom_call_target="tpu_custom_call" | custom-call | tf_op jit(solution)/shard_map/finish/pallas_call | solution.py:304
  (1 shorter events, 0.0 us)
Async XLA Ops:
  0.6 0.8 copy-start
  1.4 0.7 copy-start.1
  2.1 0.7 copy-start.2
  2.8 0.7 copy-start.3
  3.5 0.7 copy-start.4
  26.0 22.1 %collective-permute-start = (bf16[16,96,256]{2,1,0:T(8,128)(2,1)S(1)}, bf16[16,96,256]{2,1,0:T(8,128)(2,1)S(1)}, u32[]{:S(2)}, u32[]{:S(2)}) collective-permute-start(bf16[16,96,256]{2,1,0:T(8,128)(2,1)S(1)} %all_to_all.35.own.own_s), channel_id=1, source_target_pairs={{0,32},{32,0},{1,33},{33,1},{2,34},{34,2},{3,35},{35,3},{4,36},{36... | collective-permute-start | bytes 2359304 | tf_op jit(solution)/shard_map/ppermute | solution.py:236
  84.2 12.6 %collective-permute-start.1 = (f32[16,24,256]{2,1,0:T(8,128)S(1)}, f32[16,24,256]{2,1,0:T(8,128)S(1)}, u32[]{:S(2)}, u32[]{:S(2)}) collective-permute-start(f32[16,24,256]{2,1,0:T(8,128)S(1)} %all_to_all.38.own.own_i), channel_id=1, source_target_pairs={{0,32},{32,0},{1,33},{33,1},{2,34},{34,2},{3,35},{35,3},{4,36},{36... | collective-permute-start | bytes 1179656 | tf_op jit(solution)/shard_map/ppermute | solution.py:236

commit v3 on v2

--- a/solution.py
+++ b/solution.py
@@ -17,10 +17,13 @@
 GROUP_R = ("core", "z")
 GRP = 16
 DEPTH = 8
-COLS = 2 * GRP * PT
+PAIRS = DEPTH // 2
+HALF = GRP * PT
+COLS = 2 * HALF
 ROWS = DEPTH * PT
 AUG = 80
-PIECES = 8
+VMEM_ALL = 60
+PIECES = 16
 PIECE = COLS // PIECES
 
 F32 = jnp.float32
@@ -56,7 +59,19 @@
     return b / diagonal
 
 
-def prepare(emb, latent, list_of, rank_of, probes, msg_c, msg_r, resid, weight):
+def prepare(
+    emb_in, latent_in, list_in, rank_in, probes_in,
+    msg_c, emb, resid, weight,
+    latent, list_of, rank_of, probes, sems,
+):
+    pairs = (
+        (latent_in, latent), (list_in, list_of), (rank_in, rank_of), (probes_in, probes), (emb_in, emb),
+    )
+    copies = [pltpu.make_async_copy(a, b, sems.at[i]) for i, (a, b) in enumerate(pairs)]
+    for copy in copies:
+        copy.start()
+    for copy in copies[:3]:
+        copy.wait()
     row = jnp.concatenate(
         [
             latent[...],
@@ -81,6 +96,8 @@
         gradient = gradient - jnp.where(active, chance, 0.0)
         curvature = curvature + jnp.where(active, chance * (1.0 - chance), 0.0)
     w = jnp.sqrt(curvature + RIDGE)
+    copies[3].wait()
+    copies[4].wait()
     r0 = jnp.concatenate([gradient, probes[...]], axis=0)
     resid[...] = r0
     weight[...] = w
@@ -91,8 +108,6 @@
         msg_c[g, :D, :] = emb[...]
         msg_c[g, D : D + SIDES, :] = high
         msg_c[g, D + SIDES :, :] = low
-    for g in range(DEPTH):
-        msg_r[g] = emb[...]
 
 
 def norm_rows(points):
@@ -100,33 +115,45 @@
     return jnp.concatenate(split3(sq), axis=0)
 
 
-def first_apply(own, other, r_ref, out, *more):
-    tile, (left, vec) = more[:PIECES], more[PIECES:]
+def half_apply(c_ref, right, tile, left, vec):
     ones = jnp.ones((3, PT), F32)
     zeros = jnp.zeros((AUG - D - 6, PT), F32)
-    for half, ref in enumerate((own, other)):
-        for g in range(GRP):
-            at = slice((half * GRP + g) * PT, (half * GRP + g + 1) * PT)
-            points = ref[g, :D, :].astype(F32)
-            rows = jnp.concatenate([points, ones, norm_rows(points), zeros], axis=0)
-            left[at, :] = rows.astype(BF16).T
-            vec[:, at] = ref[g, D : D + SIDES, :]
-    columns = []
-    for g in range(DEPTH):
-        points = r_ref[g].astype(F32)
-        rows = [points * (2.0 * GAMMA), norm_rows(points), ones, zeros]
-        columns.append(jnp.concatenate(rows, axis=0).astype(BF16))
-    right = jnp.concatenate(columns, axis=1)
+    for g in range(GRP):
+        at = slice(g * PT, (g + 1) * PT)
+        points = c_ref[g, :D, :].astype(F32)
+        rows = jnp.concatenate([points, ones, norm_rows(points), zeros], axis=0)
+        left[at, :] = rows.astype(BF16).T
+        vec[:, at] = c_ref[g, D : D + SIDES, :]
     step = 256
     total = jnp.zeros((SIDES, ROWS), F32)
-    for j in range(COLS // step):
+    for j in range(HALF // step):
         at = slice(j * step, (j + 1) * step)
-        exponent = jnp.dot(left[at, :], right, preferred_element_type=F32)
+        exponent = jnp.dot(left[at, :], right[...], preferred_element_type=F32)
         kernel = jnp.exp(exponent).astype(BF16)
         tile[j * step // PIECE][pl.ds(j * step % PIECE, step), :] = kernel
         total += jnp.dot(vec[:, at], kernel, preferred_element_type=F32)
-    for g in range(DEPTH):
-        out[g] = total[:, g * PT : (g + 1) * PT]
+    return total
+
+
+def place_blocks(place, out, total):
+    for k in range(DEPTH):
+        out[lax.bitwise_xor(place[0], k)] = total[:, k * PT : (k + 1) * PT]
+
+
+def first_half(c_ref, *more):
+    r_refs, out, right, more = more[:PAIRS], more[PAIRS], more[PAIRS + 1], more[PAIRS + 2 :]
+    ones = jnp.ones((3, PT), F32)
+    zeros = jnp.zeros((AUG - D - 6, PT), F32)
+    for k in range(DEPTH):
+        points = r_refs[k // 2][:, k % 2 * PT : (k % 2 + 1) * PT].astype(F32)
+        rows = [points * (2.0 * GAMMA), norm_rows(points), ones, zeros]
+        right[:, k * PT : (k + 1) * PT] = jnp.concatenate(rows, axis=0).astype(BF16)
+    out[...] = half_apply(c_ref, right, more[: PIECES // 2], *more[PIECES // 2 :])
+
+
+def second_half(place, c_ref, right, before, out, *more):
+    total = half_apply(c_ref, right, more[: PIECES // 2], *more[PIECES // 2 :])
+    place_blocks(place, out, total + before[...])
 
 
 def unpack(total, n):
@@ -160,7 +187,7 @@
 
 
 def second_apply(
-    mom, own_i, other_i, own_s, other_s, res_ref, img_ref, *more
+    place, mom, own_i, other_i, own_s, other_s, res_ref, img_ref, *more
 ):
     tile, (out, sol1, res1, dir1, gram1) = more[:PIECES], more[PIECES:]
     total = jnp.sum(mom[...], axis=0)
@@ -188,8 +215,7 @@
     for j in range(len(vec)):
         kernel = tile[j * PT // PIECE][pl.ds(j * PT % PIECE, PT), :]
         total += jnp.dot(vec[j], kernel, preferred_element_type=F32)
-    for g in range(DEPTH):
-        out[g] = total[:, g * PT : (g + 1) * PT]
+    place_blocks(place, out, total)
 
 
 def second_image(parts, base, w, out, image):
@@ -199,17 +225,25 @@
     img = base[...] + w[...] * total
     image[...] = img
     gram = hdot(base[...], img, ((1,), (1,)))
+    gram = 0.5 * (gram + gram.T)
+    high = gram.astype(BF16).astype(F32)
+    rows = lax.broadcasted_iota(jnp.int32, (SIDES, SIDES), 0)
+    lanes = lax.broadcasted_iota(jnp.int32, (SIDES, SIDES), 1)
+    gram = jnp.where(rows <= lanes, high, gram - high)
     top = jnp.concatenate([gram[i : i + 1] for i in range(8)], axis=1)
     bottom = jnp.concatenate([gram[i : i + 1] for i in range(8, 16)], axis=1)
-    packed = jnp.concatenate([top, bottom], axis=0)
+    packed = jnp.concatenate([top, bottom], axis=0).astype(BF16)
     out[...] = jnp.broadcast_to(packed[None], out.shape)
 
 
 def finish(grams, gram1, sol1, res1, dir1, img1, sol, res):
-    total = jnp.sum(grams[...], axis=0)
+    total = jnp.sum(grams[...].astype(F32), axis=0)
     gram = jnp.concatenate(
         [total[i // 8 : i // 8 + 1, 16 * (i % 8) : 16 * (i % 8) + 16] for i in range(16)], axis=0
     )
+    rows = lax.broadcasted_iota(jnp.int32, (SIDES, SIDES), 0)
+    lanes = lax.broadcasted_iota(jnp.int32, (SIDES, SIDES), 1)
+    gram = gram + jnp.where(rows == lanes, 0.0, gram.T)
     step = spd_solve(gram, gram1[...])
     sol[...] = sol1[...] + hdot(step, dir1[...], ((0,), (0,)))
     res[...] = res1[...] - hdot(step, img1[...], ((0,), (0,)))
@@ -223,7 +257,7 @@
     return pl.pallas_call(
         body,
         out_shape=out,
-        compiler_params=pltpu.CompilerParams(vmem_limit_bytes=vmem << 20),
+        compiler_params=pltpu.CompilerParams(vmem_limit_bytes=int(vmem * 2**20)),
         **more,
     )
 
@@ -232,34 +266,64 @@
     return pl.BlockSpec(dims, lambda i: at or (0,) * len(dims))
 
 
+def swap_along_z(array, k):
+    return lax.ppermute(array, "z", [(i, i ^ k) for i in range(DEPTH)])
+
+
 def swap_cores(array):
     return lax.ppermute(array, "core", ((0, 1), (1, 0)))
 
 
 def per_device(embeddings, latent, list_of, rank_of, probes):
     resident = pl.BlockSpec(memory_space=pltpu.VMEM)
-    msg_c, msg_r, res0, w = call(
+    anywhere = pl.BlockSpec(memory_space=pl.ANY)
+    msg_c, points, res0, w = call(
         prepare,
         (
             shape(GRP, D + 2 * SIDES, PT, dtype=BF16),
-            shape(DEPTH, D, PT, dtype=BF16),
+            shape(D, PT, dtype=BF16),
             shape(SIDES, PT),
             shape(1, PT),
         ),
+        vmem=VMEM_ALL,
+        in_specs=[anywhere] * 5,
+        scratch_shapes=[
+            pltpu.VMEM((1, PT), F32),
+            pltpu.VMEM((1, PT), jnp.int32),
+            pltpu.VMEM((1, PT), jnp.int32),
+            pltpu.VMEM((SIDES - 1, PT), F32),
+            pltpu.SemaphoreType.DMA((5,)),
+        ],
         name="prepare",
     )(embeddings, latent[None, :], list_of[None, :], rank_of[None, :], probes)
     own_c = lax.all_to_all(msg_c, GROUP_C, 0, 0, tiled=True)
+    pair = jnp.concatenate([points, swap_along_z(points, 1)], axis=1)
+    all_r = [pair] + [swap_along_z(pair, k) for k in range(2, DEPTH, 2)]
+    own_c, all_r = lax.optimization_barrier((own_c, all_r))
     other_c = swap_cores(own_c)
-    all_r = lax.all_to_all(msg_r, "z", 0, 0, tiled=True)
-
-    part, *tile = call(
-        first_apply,
-        (shape(DEPTH, SIDES, PT), *([pltpu.VMEM((PIECE, ROWS), BF16)] * PIECES)),
-        vmem=16,
-        out_specs=(pl.BlockSpec((DEPTH, SIDES, PT), lambda: (0, 0, 0)), *([resident] * PIECES)),
-        scratch_shapes=[pltpu.VMEM((COLS, AUG), BF16), pltpu.VMEM((SIDES, COLS), BF16)],
-        name="first_apply",
-    )(own_c, other_c, all_r)
+
+    place = lax.axis_index("z").astype(jnp.int32)[None]
+    half_tile = [pltpu.VMEM((PIECE, ROWS), BF16)] * (PIECES // 2)
+    scratch = [pltpu.VMEM((HALF, AUG), BF16), pltpu.VMEM((SIDES, HALF), BF16)]
+    in_vmem = pl.BlockSpec(memory_space=pltpu.VMEM)
+    in_smem = pl.BlockSpec(memory_space=pltpu.SMEM)
+    part, right, *tile = call(
+        first_half,
+        (shape(SIDES, ROWS), shape(AUG, ROWS, dtype=BF16), *half_tile),
+        in_specs=[in_vmem] * (1 + PAIRS),
+        out_specs=[in_vmem] * (2 + PIECES // 2),
+        scratch_shapes=scratch,
+        name="first_half",
+    )(own_c, *all_r)
+    part, *more = call(
+        second_half,
+        (shape(DEPTH, SIDES, PT), *half_tile),
+        in_specs=[in_smem] + [in_vmem] * 3,
+        out_specs=[in_vmem] * (1 + PIECES // 2),
+        scratch_shapes=scratch,
+        name="second_half",
+    )(place, other_c, right, part)
+    tile = tile + more
     part = lax.all_to_all(part, "z", 0, 0, tiled=True)
 
     message, img0 = call(
@@ -289,16 +353,15 @@
             shape(SIDES, PT),
             shape(SIDES, SIDES),
         ),
-        vmem=12,
         grid=(1,),
-        in_specs=[block(GRP, 8, 128), images, images, scaled, scaled, own, own] + [resident] * PIECES,
+        in_specs=[in_smem, block(GRP, 8, 128), images, images, scaled, scaled, own, own] + [resident] * PIECES,
         out_specs=(block(DEPTH, SIDES, PT), own, own, own, block(SIDES, SIDES)),
         name="second_apply",
-    )(mom, own_i, other_i, own_c, other_c, res0, img0, *tile)
+    )(place, mom, own_i, other_i, own_c, other_c, res0, img0, *tile)
     part = lax.all_to_all(part, "z", 0, 0, tiled=True)
 
     grams, img1 = call(
-        second_image, (shape(256, 2, 128), shape(SIDES, PT)), name="second_image"
+        second_image, (shape(256, 2, 128, dtype=BF16), shape(SIDES, PT)), name="second_image"
     )(part, dir1, w)
     grams = lax.all_to_all(grams, ALL, 0, 0, tiled=True)
     return call(finish, (shape(SIDES, PT), shape(SIDES, PT)), name="finish")(

time: 140 us -> 127 us (0.907)
  blocking collectives: 105 us -> 67.4 us
  starting transfers between devices: 4.78 us -> 23.5 us
  waiting for transfers between devices: 0.01 us -> 6.18 us
  local copies, waits for them, and re-layouts: 3.5 us -> 0.81 us
  Pallas kernels: 25.9 us -> 27.9 us
    all_to_all x2 -> x0, blocking collectives: 41.2 us -> none  [the longest x1 20.9 us: per_device(): own_c = lax.all_to_all(msg_c, GROUP_C, 0, 0, tiled=True)]
    ppermute x0 -> x4, starting transfers between devices: none -> 9.65 us  [swap_along_z(): return lax.ppermute(array, 'z', [(i, i ^ k) for i in range(DEPTH)])]
    all_to_all x0 -> x1, starting transfers between devices: none -> 7.6 us  [per_device(): own_c = lax.all_to_all(msg_c, GROUP_C, 0, 0, tiled=True)]
    ppermute x0 -> x4, waiting for transfers between devices: none -> 6.17 us  [swap_along_z(): return lax.ppermute(array, 'z', [(i, i ^ k) for i in range(DEPTH)])]
    all_to_all x1, blocking collectives: 11.1 us -> 14.9 us  [per_device(): own_i = lax.all_to_all(message, GROUP_C, 0, 0, tiled=True)]
    unnamed x10 -> x5, local copies, waits for them, and re-layouts: 3.5 us -> 0.81 us
    all_to_all x2, blocking collectives: 20.7 us -> 23.1 us  [per_device(): part = lax.all_to_all(part, 'z', 0, 0, tiled=True)]
    all_to_all x1, blocking collectives: 22 us -> 19.8 us  [per_device(): grams = lax.all_to_all(grams, ALL, 0, 0, tiled=True)]
  transfers between devices with their start and end apart: 2 -> 7, of which waited for: 0 -> 2; matrix products, arithmetic and copies ran while one was open for 0% -> 1% of each run, Pallas kernels for 0% -> 6%
where the time goes in v3:
time: 127 us
  blocking collectives  67.4 us (53%)
  Pallas kernels  27.9 us (22%)
  starting transfers between devices  23.5 us (19%)
  waiting for transfers between devices  6.18 us (5%)
    all_to_all x2, blocking collectives, per_device(): part = lax.all_to_all(part, 'z', 0, 0, tiled=True)  23.1 us
    all_to_all x1, blocking collectives, per_device(): grams = lax.all_to_all(grams, ALL, 0, 0, tiled=True)  19.8 us
    all_to_all x1, blocking collectives, per_device(): own_i = lax.all_to_all(message, GROUP_C, 0, 0, tiled=True)  14.9 us
    ppermute x4, starting transfers between devices, swap_along_z(): return lax.ppermute(array, 'z', [(i, i ^ k) for i in range(DEPTH)])  9.65 us
    all_to_all x1, blocking collectives, per_device(): mom = lax.all_to_all(mom, GROUP_R, 0, 0, tiled=True)  9.62 us
    pallas_call x1, Pallas kernels, per_device(): call(second_apply, (shape(DEPTH, SIDES, PT), shape(SIDES, PT), shape(SIDE...  7.6 us
    all_to_all x1, starting transfers between devices, per_device(): own_c = lax.all_to_all(msg_c, GROUP_C, 0, 0, tiled=True)  7.6 us
    pallas_call x1, Pallas kernels, per_device(): call(second_half, (shape(DEPTH, SIDES, PT), *half_tile), in_specs=[in_sme...  7.31 us
  transfers between devices with their start and end apart: 7, of which 2 were waited for; matrix products, arithmetic and copies ran while one was open for 1% of the time, Pallas kernels for 6%

profile of v3, /device:TPU:1, one launch (start us, length us, event | category | flops | bytes accessed | tf_op | source)
XLA Modules:
  0.0 126.5 jit_solution(17935821462694214307)
XLA Ops:
  0.6 2.6 %prepare.1 = (bf16[16,96,256]{2,1,0:T(8,128)(2,1)}, bf16[64,256]{1,0:T(8,128)(2,1)}, f32[16,256]{1,0:T(8,128)}, f32[1,256]{1,0:T(1,128)}) custom-call(bf16[64,256]{1,0:T(8,128)(2,1)} %emb_in.1, f32[1,256]{1,0:T(1,128)} %bitcast.4, s32[1,256]{1,0:T(1,128)} %bitcast.5, s32[1,256]{1,0:T(1,128)} %bitcast.6, f32[15,256]{1,0:T(8,128)} %probes_in.1), custom_call_target="tpu_custom_call" | custom-call | tf_op jit(solution)/shard_map/prepare/pallas_call | solution.py:280
  3.2 0.0 copy-start
  3.3 0.0 copy-start.1
  3.3 7.6 %all-to-all-start = ((bf16[16,96,256]{2,1,0:T(8,128)(2,1)}), bf16[16,96,256]{2,1,0:T(8,128)(2,1)S(1)}, u32[]{:S(2)}, u32[]{:S(2)}) async-start(bf16[16,96,256]{2,1,0:T(8,128)(2,1)} %get-tuple-element.39), calls=%async_computation | async-start | bytes 1572864 | tf_op jit(solution)/shard_map/all_to_all | solution.py:299
  10.9 1.7 %collective-permute-start = (bf16[64,256]{1,0:T(8,128)(2,1)}, bf16[64,256]{1,0:T(8,128)(2,1)S(1)}, u32[]{:S(2)}, u32[]{:S(2)}) collective-permute-start(bf16[64,256]{1,0:T(8,128)(2,1)} %get-tuple-element.40), channel_id=1, source_target_pairs={{0,4},{4,0},{8,12},{12,8},{16,20},{20,16},{24,28},{28,24},{1,5},{5... | collective-permute-start | bytes 98312 | tf_op jit(solution)/shard_map/ppermute | solution.py:270
  12.6 0.8 constant_dynamic-update-slice_fusion.1
  13.4 0.7 collective-permute-done
  14.1 5.8 %collective-permute-start.3 = (bf16[64,512]{1,0:T(8,128)(2,1)S(1)}, bf16[64,512]{1,0:T(8,128)(2,1)S(1)}, u32[]{:S(2)}, u32[]{:S(2)}) collective-permute-start(bf16[64,512]{1,0:T(8,128)(2,1)S(1)} %constant_dynamic-update-slice_fusion.more_0_), channel_id=1, source_target_pairs={{0,24},{4,28},{8,16},{12,20},{16,8},{20,12},{24,0},{28,4},{1,25},{... | collective-permute-start | bytes 196616 | tf_op jit(solution)/shard_map/ppermute | solution.py:270
  20.0 0.9 collective-permute-start.2
  20.9 1.2 collective-permute-start.1
  22.0 0.0 collective-permute-done.3.more_3_
  22.0 5.4 %collective-permute-done.2.more_2_ = bf16[64,512]{1,0:T(8,128)(2,1)S(1)} collective-permute-done((bf16[64,512]{1,0:T(8,128)(2,1)S(1)}, bf16[64,512]{1,0:T(8,128)(2,1)S(1)}, u32[]{:S(2)}, u32[]{:S(2)}) %collective-permute-start.2) | collective-permute-done | bytes 65568 | tf_op jit(solution)/shard_map/ppermute | solution.py:270
  27.5 0.0 collective-permute-done.1.more_1_
  27.5 0.0 all-to-all-done.c_ref.own_s
  27.5 3.3 %collective-permute-start.4 = (bf16[16,96,256]{2,1,0:T(8,128)(2,1)S(1)}, bf16[16,96,256]{2,1,0:T(8,128)(2,1)S(1)}, u32[]{:S(2)}, u32[]{:S(2)}) collective-permute-start(bf16[16,96,256]{2,1,0:T(8,128)(2,1)S(1)} %all-to-all-done.c_ref.own_s), channel_id=1, source_target_pairs={{0,32},{32,0},{1,33},{33,1},{2,34},{34,2},{3,35},{35,3},{4,36},{36... | collective-permute-start | bytes 2359304 | tf_op jit(solution)/shard_map/ppermute | solution.py:274
  30.8 7.1 %first_half.1 = (f32[16,2048]{1,0:T(8,128)S(1)}, bf16[80,2048]{1,0:T(8,128)(2,1)S(1)}, bf16[512,2048]{1,0:T(8,128)(2,1)S(1)}, bf16[512,2048]{1,0:T(8,128)(2,1)S(...) custom-call(bf16[16,96,256]{2,1,0:T(8,128)(2,1)S(1)} %all-to-all-don, ...), custom_call_target="tpu_custom_call" | custom-call | tf_op jit(solution)/shard_map/first_half/pallas_call | solution.py:310
  37.9 0.0 collective-permute-done.4.c_ref.other_s
  37.9 7.3 %second_half.1 = (f32[8,16,256]{2,1,0:T(8,128)S(1)}, bf16[512,2048]{1,0:T(8,128)(2,1)S(1)}, bf16[512,2048]{1,0:T(8,128)(2,1)S(1)}, bf16[512,2048]{1,0:T(8,128)(2...) custom-call(s32[1]{0:T(128)} %bitcast.place, ...), custom_call_target="tpu_custom_call" | custom-call | tf_op jit(solution)/shard_map/second_half/pallas_call | solution.py:318
  45.2 13.0 %all_to_all.30.parts = f32[8,16,256]{2,1,0:T(8,128)S(1)} all-to-all(f32[8,16,256]{2,1,0:T(8,128)S(1)} %get-tuple-element.48), channel_id=1, replica_groups=mesh['y'=4,'core'=2,'z'=8,'x'=4] {'z'}, dimensions={0} | all-to-all | bytes 262144 | tf_op jit(solution)/shard_map/all_to_all | solution.py:327
  58.2 0.0 copy-done
  58.2 0.0 copy-done.1
  58.2 0.2 first_image.1
  58.4 14.9 %all_to_all.31.own.own_i = f32[16,24,256]{2,1,0:T(8,128)S(1)} all-to-all(f32[16,24,256]{2,1,0:T(8,128)S(1)} %get-tuple-element.51), channel_id=1, replica_groups=mesh['y'=4,'core'=2,'z'=8,'x'=4] {'y','x'}, dimensions={0} | all-to-all | bytes 786432 | tf_op jit(solution)/shard_map/all_to_all | solution.py:332
  73.4 2.9 %collective-permute-start.5 = (f32[16,24,256]{2,1,0:T(8,128)S(1)}, f32[16,24,256]{2,1,0:T(8,128)S(1)}, u32[]{:S(2)}, u32[]{:S(2)}) collective-permute-start(f32[16,24,256]{2,1,0:T(8,128)S(1)} %all_to_all.31.own.own_i), channel_id=1, source_target_pairs={{0,32},{32,0},{1,33},{33,1},{2,34},{34,2},{3,35},{35,3},{4,36},{36... | collective-permute-start | bytes 1179656 | tf_op jit(solution)/shard_map/ppermute | solution.py:274
  76.3 9.6 %all_to_all.32.mom = f32[16,8,128]{2,1,0:T(8,128)S(1)} all-to-all(f32[16,8,128]{2,1,0:T(8,128)S(1)} %gram_sum.1), channel_id=1, replica_groups=mesh['y'=4,'core'=2,'z'=8,'x'=4] {'core','z'}, dimensions={0} | all-to-all | bytes 131072 | tf_op jit(solution)/shard_map/all_to_all | solution.py:342
  85.9 0.0 collective-permute-done.5.other_i
  85.9 7.6 %second_apply.1 = (f32[8,16,256]{2,1,0:T(8,128)S(1)}, f32[16,256]{1,0:T(8,128)S(1)}, f32[16,256]{1,0:T(8,128)S(1)}, f32[16,256]{1,0:T(8,128)S(1)}, f32[16,16]{1,0:T(8,128)S(1)}) custom-call(s32[1]{0:T(128)} %bitcast.place, f32[16,8,128]{2,1,0:T(8,128)S(1)} %all_to_all.32.mom, f32[16,24,256]{2,1,0:T(8,128)S(1)} %all_to_all.31.own.own_i, ...), custom_call_target="tpu_custom_call" | custom-call | tf_op jit(solution)/shard_map/second_apply/pallas_call | solution.py:347
  93.5 10.2 %all_to_all.33.parts = f32[8,16,256]{2,1,0:T(8,128)S(1)} all-to-all(f32[8,16,256]{2,1,0:T(8,128)S(1)} %get-tuple-element.69), channel_id=1, replica_groups=mesh['y'=4,'core'=2,'z'=8,'x'=4] {'z'}, dimensions={0} | all-to-all | bytes 262144 | tf_op jit(solution)/shard_map/all_to_all | solution.py:361
  103.7 0.4 second_image.1
  104.1 19.8 %all_to_all.34.grams = bf16[256,2,128]{2,1,0:T(2,128)(2,1)S(1)} all-to-all(bf16[256,2,128]{2,1,0:T(2,128)(2,1)S(1)} %get-tuple-element.71), channel_id=1, replica_groups=mesh['y'=4,'core'=2,'z'=8,'x'=4] {'y','core','z','x'}, dimensions={0} | all-to-all | bytes 262144 | tf_op jit(solution)/shard_map/all_to_all | solution.py:366
  123.8 2.7 %finish.1 = (f32[16,256]{1,0:T(8,128)}, f32[16,256]{1,0:T(8,128)}) custom-call(bf16[256,2,128]{2,1,0:T(2,128)(2,1)S(1)} %all_to_all.34.grams, f32[16,16]{1,0:T(8,128)S(1)} %get-tuple-element.72.gram1, f32[16,256]{1,0:T(8,128)S(1)} %get-tuple-element.73.sol1, f32[16,256]{1,0:T(8,128)S(1)} %get-tuple-element.74.res1, ...), custom_call_target="tpu_custom_call" | custom-call | tf_op jit(solution)/shard_map/finish/pallas_call | solution.py:367
  (2 shorter events, 0.0 us)
Async XLA Ops:
  3.2 55.0 %copy-start = (f32[16,256]{1,0:T(8,128)S(1)}, f32[16,256]{1,0:T(8,128)}, u32[]{:S(2)}) copy-start(f32[16,256]{1,0:T(8,128)} %get-tuple-element.49.base.res_ref) | copy-start | bytes 49156
  3.3 55.0 %copy-start.1 = (f32[1,256]{1,0:T(1,128)S(1)}, f32[1,256]{1,0:T(1,128)}, u32[]{:S(2)}) copy-start(f32[1,256]{1,0:T(1,128)} %get-tuple-element.50.w) | copy-start | bytes 3076
  3.3 24.2 %all-to-all-start = ((bf16[16,96,256]{2,1,0:T(8,128)(2,1)}), bf16[16,96,256]{2,1,0:T(8,128)(2,1)S(1)}, u32[]{:S(2)}, u32[]{:S(2)}) async-start(bf16[16,96,256]{2,1,0:T(8,128)(2,1)} %get-tuple-element.39), calls=%async_computation | async-start | bytes 1572864 | tf_op jit(solution)/shard_map/all_to_all | solution.py:299
  10.9 3.2 %collective-permute-start = (bf16[64,256]{1,0:T(8,128)(2,1)}, bf16[64,256]{1,0:T(8,128)(2,1)S(1)}, u32[]{:S(2)}, u32[]{:S(2)}) collective-permute-start(bf16[64,256]{1,0:T(8,128)(2,1)} %get-tuple-element.40), channel_id=1, source_target_pairs={{0,4},{4,0},{8,12},{12,8},{16,20},{20,16},{24,28},{28,24},{1,5},{5... | collective-permute-start | bytes 98312 | tf_op jit(solution)/shard_map/ppermute | solution.py:270
  14.1 7.9 %collective-permute-start.3 = (bf16[64,512]{1,0:T(8,128)(2,1)S(1)}, bf16[64,512]{1,0:T(8,128)(2,1)S(1)}, u32[]{:S(2)}, u32[]{:S(2)}) collective-permute-start(bf16[64,512]{1,0:T(8,128)(2,1)S(1)} %constant_dynamic-update-slice_fusion.more_0_), channel_id=1, source_target_pairs={{0,24},{4,28},{8,16},{12,20},{16,8},{20,12},{24,0},{28,4},{1,25},{... | collective-permute-start | bytes 196616 | tf_op jit(solution)/shard_map/ppermute | solution.py:270
  20.0 7.5 %collective-permute-start.2 = (bf16[64,512]{1,0:T(8,128)(2,1)S(1)}, bf16[64,512]{1,0:T(8,128)(2,1)S(1)}, u32[]{:S(2)}, u32[]{:S(2)}) collective-permute-start(bf16[64,512]{1,0:T(8,128)(2,1)S(1)} %constant_dynamic-update-slice_fusion.more_0_), channel_id=1, source_target_pairs={{0,16},{4,20},{8,24},{12,28},{16,0},{20,4},{24,8},{28,12},{1,17},{... | collective-permute-start | bytes 196616 | tf_op jit(solution)/shard_map/ppermute | solution.py:270
  20.9 6.6 %collective-permute-start.1 = (bf16[64,512]{1,0:T(8,128)(2,1)S(1)}, bf16[64,512]{1,0:T(8,128)(2,1)S(1)}, u32[]{:S(2)}, u32[]{:S(2)}) collective-permute-start(bf16[64,512]{1,0:T(8,128)(2,1)S(1)} %constant_dynamic-update-slice_fusion.more_0_), channel_id=1, source_target_pairs={{0,8},{4,12},{8,0},{12,4},{16,24},{20,28},{24,16},{28,20},{1,9},{5... | collective-permute-start | bytes 196616 | tf_op jit(solution)/shard_map/ppermute | solution.py:270
  27.5 10.4 %collective-permute-start.4 = (bf16[16,96,256]{2,1,0:T(8,128)(2,1)S(1)}, bf16[16,96,256]{2,1,0:T(8,128)(2,1)S(1)}, u32[]{:S(2)}, u32[]{:S(2)}) collective-permute-start(bf16[16,96,256]{2,1,0:T(8,128)(2,1)S(1)} %all-to-all-done.c_ref.own_s), channel_id=1, source_target_pairs={{0,32},{32,0},{1,33},{33,1},{2,34},{34,2},{3,35},{35,3},{4,36},{36... | collective-permute-start | bytes 2359304 | tf_op jit(solution)/shard_map/ppermute | solution.py:274
  73.4 12.6 %collective-permute-start.5 = (f32[16,24,256]{2,1,0:T(8,128)S(1)}, f32[16,24,256]{2,1,0:T(8,128)S(1)}, u32[]{:S(2)}, u32[]{:S(2)}) collective-permute-start(f32[16,24,256]{2,1,0:T(8,128)S(1)} %all_to_all.31.own.own_i), channel_id=1, source_target_pairs={{0,32},{32,0},{1,33},{33,1},{2,34},{34,2},{3,35},{35,3},{4,36},{36... | collective-permute-start | bytes 1179656 | tf_op jit(solution)/shard_map/ppermute | solution.py:274

commit v4 on v3

--- a/solution.py
+++ b/solution.py
@@ -45,18 +45,19 @@
 
 def spd_solve(gram, right):
     n = gram.shape[0]
-    lanes = lax.broadcasted_iota(jnp.int32, (n, n), 1)
-    rows = lax.broadcasted_iota(jnp.int32, (n, n), 0)
-    a, b = 0.5 * (gram + gram.T), right
+    rows = lax.broadcasted_iota(jnp.int32, right.shape, 0)
+    gram = 0.5 * (gram + gram.T)
+    columns = [jnp.broadcast_to(gram[:, k : k + 1], right.shape) for k in range(n)]
+    diagonal = jnp.ones(right.shape, F32)
     for k in range(n):
-        pivot = a[k : k + 1, k : k + 1]
-        column = a[:, k : k + 1]
-        factor = jnp.where(rows[:, :1] == k, 0.0, column / pivot)
-        a_row, b_row = a[k : k + 1, :], b[k : k + 1, :]
-        a = a - factor * a_row
-        b = b - factor * b_row
-    diagonal = jnp.sum(jnp.where(lanes == rows, a, 0.0), axis=1, keepdims=True)
-    return b / diagonal
+        pivot = columns[k][k : k + 1, :]
+        scale = 1.0 / pivot
+        factor = jnp.where(rows == k, 0.0, columns[k])
+        diagonal = jnp.where(rows == k, scale, diagonal)
+        for j in range(k + 1, n):
+            columns[j] = columns[j] - factor * (columns[j][k : k + 1, :] * scale)
+        right = right - factor * (right[k : k + 1, :] * scale)
+    return right * diagonal
 
 
 def prepare(

time: 127 us -> 125 us (0.984)
  Pallas kernels: 27.9 us -> 25.4 us
    pallas_call x1, Pallas kernels: 7.6 us -> 6.19 us  [per_device(): call(second_apply, (shape(DEPTH, SIDES, PT), shape(SIDES, PT), shape(SIDE...]
where the time goes in v4:
time: 125 us; the launch traced here: 124 us
  blocking collectives  67.4 us (54%)
  Pallas kernels  25.4 us (20%)
  starting transfers between devices  23.5 us (19%)
  waiting for transfers between devices  6.18 us (5%)
    all_to_all x2, blocking collectives, per_device(): part = lax.all_to_all(part, 'z', 0, 0, tiled=True)  23.1 us
    all_to_all x1, blocking collectives, per_device(): grams = lax.all_to_all(grams, ALL, 0, 0, tiled=True)  19.8 us
    all_to_all x1, blocking collectives, per_device(): own_i = lax.all_to_all(message, GROUP_C, 0, 0, tiled=True)  14.9 us
    ppermute x4, starting transfers between devices, swap_along_z(): return lax.ppermute(array, 'z', [(i, i ^ k) for i in range(DEPTH)])  9.65 us
    all_to_all x1, blocking collectives, per_device(): mom = lax.all_to_all(mom, GROUP_R, 0, 0, tiled=True)  9.62 us
    all_to_all x1, starting transfers between devices, per_device(): own_c = lax.all_to_all(msg_c, GROUP_C, 0, 0, tiled=True)  7.6 us
    pallas_call x1, Pallas kernels, per_device(): call(second_half, (shape(DEPTH, SIDES, PT), *half_tile), in_specs=[in_sme...  7.31 us
    pallas_call x1, Pallas kernels, per_device(): call(first_half, (shape(SIDES, ROWS), shape(AUG, ROWS, dtype=BF16), *half...  7.08 us
  transfers between devices with their start and end apart: 7, of which 2 were waited for; matrix products, arithmetic and copies ran while one was open for 1% of the time, Pallas kernels for 6%

profile of v4, /device:TPU:1, one launch (start us, length us, event | category | flops | bytes accessed | tf_op | source)
XLA Modules:
  0.0 124.0 jit_solution(7817190010426204997)
XLA Ops:
  0.6 2.6 %prepare.1 = (bf16[16,96,256]{2,1,0:T(8,128)(2,1)}, bf16[64,256]{1,0:T(8,128)(2,1)}, f32[16,256]{1,0:T(8,128)}, f32[1,256]{1,0:T(1,128)}) custom-call(bf16[64,256]{1,0:T(8,128)(2,1)} %emb_in.1, f32[1,256]{1,0:T(1,128)} %bitcast.4, s32[1,256]{1,0:T(1,128)} %bitcast.5, s32[1,256]{1,0:T(1,128)} %bitcast.6, f32[15,256]{1,0:T(8,128)} %probes_in.1), custom_call_target="tpu_custom_call" | custom-call | tf_op jit(solution)/shard_map/prepare/pallas_call | solution.py:281
  3.2 0.0 copy-start
  3.3 0.0 copy-start.1
  3.3 7.6 %all-to-all-start = ((bf16[16,96,256]{2,1,0:T(8,128)(2,1)}), bf16[16,96,256]{2,1,0:T(8,128)(2,1)S(1)}, u32[]{:S(2)}, u32[]{:S(2)}) async-start(bf16[16,96,256]{2,1,0:T(8,128)(2,1)} %get-tuple-element.39), calls=%async_computation | async-start | bytes 1572864 | tf_op jit(solution)/shard_map/all_to_all | solution.py:300
  10.9 1.7 %collective-permute-start = (bf16[64,256]{1,0:T(8,128)(2,1)}, bf16[64,256]{1,0:T(8,128)(2,1)S(1)}, u32[]{:S(2)}, u32[]{:S(2)}) collective-permute-start(bf16[64,256]{1,0:T(8,128)(2,1)} %get-tuple-element.40), channel_id=1, source_target_pairs={{0,4},{4,0},{8,12},{12,8},{16,20},{20,16},{24,28},{28,24},{1,5},{5... | collective-permute-start | bytes 98312 | tf_op jit(solution)/shard_map/ppermute | solution.py:271
  12.6 0.8 constant_dynamic-update-slice_fusion.1
  13.4 0.7 collective-permute-done
  14.1 5.8 %collective-permute-start.3 = (bf16[64,512]{1,0:T(8,128)(2,1)S(1)}, bf16[64,512]{1,0:T(8,128)(2,1)S(1)}, u32[]{:S(2)}, u32[]{:S(2)}) collective-permute-start(bf16[64,512]{1,0:T(8,128)(2,1)S(1)} %constant_dynamic-update-slice_fusion.more_0_), channel_id=1, source_target_pairs={{0,24},{4,28},{8,16},{12,20},{16,8},{20,12},{24,0},{28,4},{1,25},{... | collective-permute-start | bytes 196616 | tf_op jit(solution)/shard_map/ppermute | solution.py:271
  20.0 0.9 collective-permute-start.2
  20.9 1.2 collective-permute-start.1
  22.0 0.0 collective-permute-done.3.more_3_
  22.0 5.4 %collective-permute-done.2.more_2_ = bf16[64,512]{1,0:T(8,128)(2,1)S(1)} collective-permute-done((bf16[64,512]{1,0:T(8,128)(2,1)S(1)}, bf16[64,512]{1,0:T(8,128)(2,1)S(1)}, u32[]{:S(2)}, u32[]{:S(2)}) %collective-permute-start.2) | collective-permute-done | bytes 65568 | tf_op jit(solution)/shard_map/ppermute | solution.py:271
  27.5 0.0 collective-permute-done.1.more_1_
  27.5 0.0 all-to-all-done.c_ref.own_s
  27.5 3.3 %collective-permute-start.4 = (bf16[16,96,256]{2,1,0:T(8,128)(2,1)S(1)}, bf16[16,96,256]{2,1,0:T(8,128)(2,1)S(1)}, u32[]{:S(2)}, u32[]{:S(2)}) collective-permute-start(bf16[16,96,256]{2,1,0:T(8,128)(2,1)S(1)} %all-to-all-done.c_ref.own_s), channel_id=1, source_target_pairs={{0,32},{32,0},{1,33},{33,1},{2,34},{34,2},{3,35},{35,3},{4,36},{36... | collective-permute-start | bytes 2359304 | tf_op jit(solution)/shard_map/ppermute | solution.py:275
  30.8 7.1 %first_half.1 = (f32[16,2048]{1,0:T(8,128)S(1)}, bf16[80,2048]{1,0:T(8,128)(2,1)S(1)}, bf16[512,2048]{1,0:T(8,128)(2,1)S(1)}, bf16[512,2048]{1,0:T(8,128)(2,1)S(...) custom-call(bf16[16,96,256]{2,1,0:T(8,128)(2,1)S(1)} %all-to-all-don, ...), custom_call_target="tpu_custom_call" | custom-call | tf_op jit(solution)/shard_map/first_half/pallas_call | solution.py:311
  37.9 0.0 collective-permute-done.4.c_ref.other_s
  37.9 7.3 %second_half.1 = (f32[8,16,256]{2,1,0:T(8,128)S(1)}, bf16[512,2048]{1,0:T(8,128)(2,1)S(1)}, bf16[512,2048]{1,0:T(8,128)(2,1)S(1)}, bf16[512,2048]{1,0:T(8,128)(2...) custom-call(s32[1]{0:T(128)} %bitcast.place, ...), custom_call_target="tpu_custom_call" | custom-call | tf_op jit(solution)/shard_map/second_half/pallas_call | solution.py:319
  45.2 13.0 %all_to_all.30.parts = f32[8,16,256]{2,1,0:T(8,128)S(1)} all-to-all(f32[8,16,256]{2,1,0:T(8,128)S(1)} %get-tuple-element.48), channel_id=1, replica_groups=mesh['y'=4,'core'=2,'z'=8,'x'=4] {'z'}, dimensions={0} | all-to-all | bytes 262144 | tf_op jit(solution)/shard_map/all_to_all | solution.py:328
  58.2 0.0 copy-done
  58.2 0.0 copy-done.1
  58.2 0.2 first_image.1
  58.4 14.9 %all_to_all.31.own.own_i = f32[16,24,256]{2,1,0:T(8,128)S(1)} all-to-all(f32[16,24,256]{2,1,0:T(8,128)S(1)} %get-tuple-element.51), channel_id=1, replica_groups=mesh['y'=4,'core'=2,'z'=8,'x'=4] {'y','x'}, dimensions={0} | all-to-all | bytes 786432 | tf_op jit(solution)/shard_map/all_to_all | solution.py:333
  73.4 2.9 %collective-permute-start.5 = (f32[16,24,256]{2,1,0:T(8,128)S(1)}, f32[16,24,256]{2,1,0:T(8,128)S(1)}, u32[]{:S(2)}, u32[]{:S(2)}) collective-permute-start(f32[16,24,256]{2,1,0:T(8,128)S(1)} %all_to_all.31.own.own_i), channel_id=1, source_target_pairs={{0,32},{32,0},{1,33},{33,1},{2,34},{34,2},{3,35},{35,3},{4,36},{36... | collective-permute-start | bytes 1179656 | tf_op jit(solution)/shard_map/ppermute | solution.py:275
  76.3 9.6 %all_to_all.32.mom = f32[16,8,128]{2,1,0:T(8,128)S(1)} all-to-all(f32[16,8,128]{2,1,0:T(8,128)S(1)} %gram_sum.1), channel_id=1, replica_groups=mesh['y'=4,'core'=2,'z'=8,'x'=4] {'core','z'}, dimensions={0} | all-to-all | bytes 131072 | tf_op jit(solution)/shard_map/all_to_all | solution.py:343
  85.9 0.0 collective-permute-done.5.other_i
  85.9 6.2 %second_apply.1 = (f32[8,16,256]{2,1,0:T(8,128)S(1)}, f32[16,256]{1,0:T(8,128)S(1)}, f32[16,256]{1,0:T(8,128)S(1)}, f32[16,256]{1,0:T(8,128)S(1)}, f32[16,16]{1,0:T(8,128)S(1)}) custom-call(s32[1]{0:T(128)} %bitcast.place, f32[16,8,128]{2,1,0:T(8,128)S(1)} %all_to_all.32.mom, f32[16,24,256]{2,1,0:T(8,128)S(1)} %all_to_all.31.own.own_i, ...), custom_call_target="tpu_custom_call" | custom-call | tf_op jit(solution)/shard_map/second_apply/pallas_call | solution.py:348
  92.1 10.2 %all_to_all.33.parts = f32[8,16,256]{2,1,0:T(8,128)S(1)} all-to-all(f32[8,16,256]{2,1,0:T(8,128)S(1)} %get-tuple-element.69), channel_id=1, replica_groups=mesh['y'=4,'core'=2,'z'=8,'x'=4] {'z'}, dimensions={0} | all-to-all | bytes 262144 | tf_op jit(solution)/shard_map/all_to_all | solution.py:362
  102.3 0.4 second_image.1
  102.7 19.8 %all_to_all.34.grams = bf16[256,2,128]{2,1,0:T(2,128)(2,1)S(1)} all-to-all(bf16[256,2,128]{2,1,0:T(2,128)(2,1)S(1)} %get-tuple-element.71), channel_id=1, replica_groups=mesh['y'=4,'core'=2,'z'=8,'x'=4] {'y','core','z','x'}, dimensions={0} | all-to-all | bytes 262144 | tf_op jit(solution)/shard_map/all_to_all | solution.py:367
  122.4 1.6 %finish.1 = (f32[16,256]{1,0:T(8,128)}, f32[16,256]{1,0:T(8,128)}) custom-call(bf16[256,2,128]{2,1,0:T(2,128)(2,1)S(1)} %all_to_all.34.grams, f32[16,16]{1,0:T(8,128)S(1)} %get-tuple-element.72.gram1, f32[16,256]{1,0:T(8,128)S(1)} %get-tuple-element.73.sol1, f32[16,256]{1,0:T(8,128)S(1)} %get-tuple-element.74.res1, ...), custom_call_target="tpu_custom_call" | custom-call | tf_op jit(solution)/shard_map/finish/pallas_call | solution.py:368
  (2 shorter events, 0.0 us)
Async XLA Ops:
  3.2 55.0 %copy-start = (f32[16,256]{1,0:T(8,128)S(1)}, f32[16,256]{1,0:T(8,128)}, u32[]{:S(2)}) copy-start(f32[16,256]{1,0:T(8,128)} %get-tuple-element.49.base.res_ref) | copy-start | bytes 49156
  3.3 55.0 %copy-start.1 = (f32[1,256]{1,0:T(1,128)S(1)}, f32[1,256]{1,0:T(1,128)}, u32[]{:S(2)}) copy-start(f32[1,256]{1,0:T(1,128)} %get-tuple-element.50.w) | copy-start | bytes 3076
  3.3 24.2 %all-to-all-start = ((bf16[16,96,256]{2,1,0:T(8,128)(2,1)}), bf16[16,96,256]{2,1,0:T(8,128)(2,1)S(1)}, u32[]{:S(2)}, u32[]{:S(2)}) async-start(bf16[16,96,256]{2,1,0:T(8,128)(2,1)} %get-tuple-element.39), calls=%async_computation | async-start | bytes 1572864 | tf_op jit(solution)/shard_map/all_to_all | solution.py:300
  10.9 3.2 %collective-permute-start = (bf16[64,256]{1,0:T(8,128)(2,1)}, bf16[64,256]{1,0:T(8,128)(2,1)S(1)}, u32[]{:S(2)}, u32[]{:S(2)}) collective-permute-start(bf16[64,256]{1,0:T(8,128)(2,1)} %get-tuple-element.40), channel_id=1, source_target_pairs={{0,4},{4,0},{8,12},{12,8},{16,20},{20,16},{24,28},{28,24},{1,5},{5... | collective-permute-start | bytes 98312 | tf_op jit(solution)/shard_map/ppermute | solution.py:271
  14.1 7.9 %collective-permute-start.3 = (bf16[64,512]{1,0:T(8,128)(2,1)S(1)}, bf16[64,512]{1,0:T(8,128)(2,1)S(1)}, u32[]{:S(2)}, u32[]{:S(2)}) collective-permute-start(bf16[64,512]{1,0:T(8,128)(2,1)S(1)} %constant_dynamic-update-slice_fusion.more_0_), channel_id=1, source_target_pairs={{0,24},{4,28},{8,16},{12,20},{16,8},{20,12},{24,0},{28,4},{1,25},{... | collective-permute-start | bytes 196616 | tf_op jit(solution)/shard_map/ppermute | solution.py:271
  20.0 7.5 %collective-permute-start.2 = (bf16[64,512]{1,0:T(8,128)(2,1)S(1)}, bf16[64,512]{1,0:T(8,128)(2,1)S(1)}, u32[]{:S(2)}, u32[]{:S(2)}) collective-permute-start(bf16[64,512]{1,0:T(8,128)(2,1)S(1)} %constant_dynamic-update-slice_fusion.more_0_), channel_id=1, source_target_pairs={{0,16},{4,20},{8,24},{12,28},{16,0},{20,4},{24,8},{28,12},{1,17},{... | collective-permute-start | bytes 196616 | tf_op jit(solution)/shard_map/ppermute | solution.py:271
  20.9 6.6 %collective-permute-start.1 = (bf16[64,512]{1,0:T(8,128)(2,1)S(1)}, bf16[64,512]{1,0:T(8,128)(2,1)S(1)}, u32[]{:S(2)}, u32[]{:S(2)}) collective-permute-start(bf16[64,512]{1,0:T(8,128)(2,1)S(1)} %constant_dynamic-update-slice_fusion.more_0_), channel_id=1, source_target_pairs={{0,8},{4,12},{8,0},{12,4},{16,24},{20,28},{24,16},{28,20},{1,9},{5... | collective-permute-start | bytes 196616 | tf_op jit(solution)/shard_map/ppermute | solution.py:271
  27.5 10.4 %collective-permute-start.4 = (bf16[16,96,256]{2,1,0:T(8,128)(2,1)S(1)}, bf16[16,96,256]{2,1,0:T(8,128)(2,1)S(1)}, u32[]{:S(2)}, u32[]{:S(2)}) collective-permute-start(bf16[16,96,256]{2,1,0:T(8,128)(2,1)S(1)} %all-to-all-done.c_ref.own_s), channel_id=1, source_target_pairs={{0,32},{32,0},{1,33},{33,1},{2,34},{34,2},{3,35},{35,3},{4,36},{36... | collective-permute-start | bytes 2359304 | tf_op jit(solution)/shard_map/ppermute | solution.py:275
  73.4 12.6 %collective-permute-start.5 = (f32[16,24,256]{2,1,0:T(8,128)S(1)}, f32[16,24,256]{2,1,0:T(8,128)S(1)}, u32[]{:S(2)}, u32[]{:S(2)}) collective-permute-start(f32[16,24,256]{2,1,0:T(8,128)S(1)} %all_to_all.31.own.own_i), channel_id=1, source_target_pairs={{0,32},{32,0},{1,33},{33,1},{2,34},{34,2},{3,35},{35,3},{4,36},{36... | collective-permute-start | bytes 1179656 | tf_op jit(solution)/shard_map/ppermute | solution.py:275

commit v5 on v4

--- a/solution.py
+++ b/solution.py
@@ -14,7 +14,7 @@
 GAMMA = 2.0 / D
 ALL = ("y", "core", "z", "x")
 GROUP_C = ("y", "x")
-GROUP_R = ("core", "z")
+GROUP_LAST = ("y", "core", "x")
 GRP = 16
 DEPTH = 8
 PAIRS = DEPTH // 2
@@ -62,8 +62,8 @@
 
 def prepare(
     emb_in, latent_in, list_in, rank_in, probes_in,
-    msg_c, emb, resid, weight,
-    latent, list_of, rank_of, probes, sems,
+    msg_c, scaled_own, resid, weight,
+    emb, latent, list_of, rank_of, probes, sems,
 ):
     pairs = (
         (latent_in, latent), (list_in, list_of), (rank_in, rank_of), (probes_in, probes), (emb_in, emb),
@@ -105,6 +105,7 @@
     scaled = w * r0
     high = scaled.astype(BF16)
     low = (scaled - high.astype(F32)).astype(BF16)
+    scaled_own[...] = high
     for g in range(GRP):
         msg_c[g, :D, :] = emb[...]
         msg_c[g, D : D + SIDES, :] = high
@@ -136,11 +137,6 @@
     return total
 
 
-def place_blocks(place, out, total):
-    for k in range(DEPTH):
-        out[lax.bitwise_xor(place[0], k)] = total[:, k * PT : (k + 1) * PT]
-
-
 def first_half(c_ref, *more):
     r_refs, out, right, more = more[:PAIRS], more[PAIRS], more[PAIRS + 1], more[PAIRS + 2 :]
     ones = jnp.ones((3, PT), F32)
@@ -154,7 +150,9 @@
 
 def second_half(place, c_ref, right, before, out, *more):
     total = half_apply(c_ref, right, more[: PIECES // 2], *more[PIECES // 2 :])
-    place_blocks(place, out, total + before[...])
+    total = total + before[...]
+    for k in range(DEPTH):
+        out[lax.bitwise_xor(place[0], k)] = total[:, k * PT : (k + 1) * PT]
 
 
 def unpack(total, n):
@@ -163,7 +161,7 @@
     )
 
 
-def first_image(parts, base, w, out, image):
+def first_image(parts, base, w, out, image, weighted):
     total = parts[0]
     for g in range(1, DEPTH):
         total = total + parts[g]
@@ -174,24 +172,34 @@
     gram = hdot(both, both, ((1,), (1,)))
     rr, ri, ii = gram[:SIDES, :SIDES], gram[:SIDES, SIDES:], gram[SIDES:, SIDES:]
     packed = [rr[:8], rr[8:], ri[:8], ri[8:], ii[:8], ii[8:], jnp.zeros((8, 160), F32)]
+    weighted[...] = w[...] * i0
     message = jnp.concatenate([w[...] * i0, jnp.concatenate(packed, axis=1)], axis=0)
     for g in range(GRP):
         out[g] = message
 
 
-def gram_sum(own, out):
-    total = own[0]
+def gram_sum(own, other, scaled, weighted, out):
+    total = own[0] + other[0]
     for g in range(1, GRP):
-        total = total + own[g]
-    for g in range(GRP):
-        out[g] = total
-
-
-def second_apply(
-    place, mom, own_i, other_i, own_s, other_s, res_ref, img_ref, *more
-):
+        total = total + (own[g] + other[g])
+    high, mid, low = split3(total)
+    grams = [
+        jnp.concatenate([high, mid], axis=1),
+        jnp.concatenate([low, jnp.zeros((8, PT - 128), F32)], axis=1),
+    ]
+    message = jnp.concatenate([weighted[...]] + grams, axis=0).astype(BF16)
+    for g in range(DEPTH):
+        out[g, :SIDES, :] = scaled[...]
+        out[g, SIDES:, :] = message
+
+
+def second_apply(place, along_z, own_i, other_i, own_s, other_s, *more):
+    (res_ref, img_ref), more = more[:2], more[2:]
     tile, (out, sol1, res1, dir1, gram1) = more[:PIECES], more[PIECES:]
-    total = jnp.sum(mom[...], axis=0)
+    total = along_z[0, 2 * SIDES :, :].astype(F32)
+    for g in range(1, DEPTH):
+        total = total + along_z[g, 2 * SIDES :, :].astype(F32)
+    total = total[:8, :128] + (total[:8, 128:] + total[8:, :128])
     rr, ri, ii = unpack(total, 0), unpack(total, 1), unpack(total, 2)
     step = spd_solve(ri, rr)
     cross = hdot(step, ri, ((0,), (1,)))
@@ -202,7 +210,8 @@
     sol1[...] = hdot(step, r0, ((0,), (0,)))
     r1 = r0 - hdot(step, i0, ((0,), (0,)))
     res1[...] = r1
-    dir1[...] = r1 + hdot(mix, r0, ((0,), (0,)))
+    d1 = r1 + hdot(mix, r0, ((0,), (0,)))
+    dir1[...] = d1
     rows = lax.broadcasted_iota(jnp.int32, (SIDES, SIDES), 0)
     lanes = lax.broadcasted_iota(jnp.int32, (SIDES, SIDES), 1)
     coef = jnp.concatenate([jnp.where(rows == lanes, 1.0, 0.0) + mix, -step], axis=0)
@@ -216,35 +225,35 @@
     for j in range(len(vec)):
         kernel = tile[j * PT // PIECE][pl.ds(j * PT % PIECE, PT), :]
         total += jnp.dot(vec[j], kernel, preferred_element_type=F32)
-    place_blocks(place, out, total)
+    weighted = []
+    for k in range(DEPTH):
+        both = along_z[lax.bitwise_xor(place[0], k), : 2 * SIDES, :].astype(F32)
+        weighted.append(hdot(coef, both, ((0,), (0,))))
+    gram = hdot(d1, d1, ((1,), (1,)))
+    gram = gram + hdot(jnp.concatenate(weighted, axis=1), total, ((1,), (1,)))
+    gram = jnp.concatenate([gram[:8], gram[8:], jnp.zeros((8, PT - 32), F32)], axis=1)
+    for k in range(DEPTH):
+        part = total[:, k * PT : (k + 1) * PT]
+        out[lax.bitwise_xor(place[0], k)] = jnp.concatenate([part, gram], axis=0)
 
 
 def second_image(parts, base, w, out, image):
     total = parts[0]
     for g in range(1, DEPTH):
         total = total + parts[g]
-    img = base[...] + w[...] * total
-    image[...] = img
-    gram = hdot(base[...], img, ((1,), (1,)))
-    gram = 0.5 * (gram + gram.T)
-    high = gram.astype(BF16).astype(F32)
-    rows = lax.broadcasted_iota(jnp.int32, (SIDES, SIDES), 0)
-    lanes = lax.broadcasted_iota(jnp.int32, (SIDES, SIDES), 1)
-    gram = jnp.where(rows <= lanes, high, gram - high)
+    image[...] = base[...] + w[...] * total[:SIDES]
+    gram = unpack(total[SIDES:], 0)
     top = jnp.concatenate([gram[i : i + 1] for i in range(8)], axis=1)
     bottom = jnp.concatenate([gram[i : i + 1] for i in range(8, 16)], axis=1)
-    packed = jnp.concatenate([top, bottom], axis=0).astype(BF16)
+    packed = jnp.concatenate([top, bottom], axis=0)
     out[...] = jnp.broadcast_to(packed[None], out.shape)
 
 
 def finish(grams, gram1, sol1, res1, dir1, img1, sol, res):
-    total = jnp.sum(grams[...].astype(F32), axis=0)
+    total = jnp.sum(grams[...], axis=0)
     gram = jnp.concatenate(
         [total[i // 8 : i // 8 + 1, 16 * (i % 8) : 16 * (i % 8) + 16] for i in range(16)], axis=0
     )
-    rows = lax.broadcasted_iota(jnp.int32, (SIDES, SIDES), 0)
-    lanes = lax.broadcasted_iota(jnp.int32, (SIDES, SIDES), 1)
-    gram = gram + jnp.where(rows == lanes, 0.0, gram.T)
     step = spd_solve(gram, gram1[...])
     sol[...] = sol1[...] + hdot(step, dir1[...], ((0,), (0,)))
     res[...] = res1[...] - hdot(step, img1[...], ((0,), (0,)))
@@ -278,17 +287,18 @@
 def per_device(embeddings, latent, list_of, rank_of, probes):
     resident = pl.BlockSpec(memory_space=pltpu.VMEM)
     anywhere = pl.BlockSpec(memory_space=pl.ANY)
-    msg_c, points, res0, w = call(
+    msg_c, scaled_own, res0, w = call(
         prepare,
         (
             shape(GRP, D + 2 * SIDES, PT, dtype=BF16),
-            shape(D, PT, dtype=BF16),
+            shape(SIDES, PT, dtype=BF16),
             shape(SIDES, PT),
             shape(1, PT),
         ),
         vmem=VMEM_ALL,
         in_specs=[anywhere] * 5,
         scratch_shapes=[
+            pltpu.VMEM((D, PT), BF16),
             pltpu.VMEM((1, PT), F32),
             pltpu.VMEM((1, PT), jnp.int32),
             pltpu.VMEM((1, PT), jnp.int32),
@@ -298,7 +308,7 @@
         name="prepare",
     )(embeddings, latent[None, :], list_of[None, :], rank_of[None, :], probes)
     own_c = lax.all_to_all(msg_c, GROUP_C, 0, 0, tiled=True)
-    pair = jnp.concatenate([points, swap_along_z(points, 1)], axis=1)
+    pair = jnp.concatenate([embeddings, swap_along_z(embeddings, 1)], axis=1)
     all_r = [pair] + [swap_along_z(pair, k) for k in range(2, DEPTH, 2)]
     own_c, all_r = lax.optimization_barrier((own_c, all_r))
     other_c = swap_cores(own_c)
@@ -327,44 +337,49 @@
     tile = tile + more
     part = lax.all_to_all(part, "z", 0, 0, tiled=True)
 
-    message, img0 = call(
-        first_image, (shape(GRP, SIDES + 8, PT), shape(SIDES, PT)), name="first_image"
+    message, img0, weighted = call(
+        first_image,
+        (shape(GRP, SIDES + 8, PT), shape(SIDES, PT), shape(SIDES, PT)),
+        name="first_image",
     )(part, res0, w)
     own_i = lax.all_to_all(message, GROUP_C, 0, 0, tiled=True)
     other_i = swap_cores(own_i)
-    mom = call(
+    grams = block(GRP, 8, 128, at=(0, 2, 0))
+    own = block(SIDES, PT)
+    along_z = call(
         gram_sum,
-        shape(GRP, 8, 128),
+        shape(DEPTH, 3 * SIDES, PT, dtype=BF16),
         grid=(1,),
-        in_specs=[block(GRP, 8, 128, at=(0, 2, 0))],
-        out_specs=block(GRP, 8, 128),
+        in_specs=[grams, grams, own, own],
+        out_specs=block(DEPTH, 3 * SIDES, PT),
         name="gram_sum",
-    )(own_i)
-    mom = lax.all_to_all(mom, GROUP_R, 0, 0, tiled=True)
+    )(own_i, other_i, scaled_own, weighted)
+    along_z = lax.all_to_all(along_z, "z", 0, 0, tiled=True)
 
     images = block(GRP, SIDES, PT)
     scaled = block(GRP, 2 * SIDES, PT, at=(0, 2, 0))
-    own = block(SIDES, PT)
     part, sol1, res1, dir1, gram1 = call(
         second_apply,
         (
-            shape(DEPTH, SIDES, PT),
+            shape(DEPTH, SIDES + 8, PT),
             shape(SIDES, PT),
             shape(SIDES, PT),
             shape(SIDES, PT),
             shape(SIDES, SIDES),
         ),
         grid=(1,),
-        in_specs=[in_smem, block(GRP, 8, 128), images, images, scaled, scaled, own, own] + [resident] * PIECES,
-        out_specs=(block(DEPTH, SIDES, PT), own, own, own, block(SIDES, SIDES)),
+        in_specs=[in_smem, block(DEPTH, 3 * SIDES, PT)]
+        + [images, images, scaled, scaled]
+        + [own, own] + [resident] * PIECES,
+        out_specs=(block(DEPTH, SIDES + 8, PT), own, own, own, block(SIDES, SIDES)),
         name="second_apply",
-    )(place, mom, own_i, other_i, own_c, other_c, res0, img0, *tile)
+    )(place, along_z, own_i, other_i, own_c, other_c, res0, img0, *tile)
     part = lax.all_to_all(part, "z", 0, 0, tiled=True)
 
     grams, img1 = call(
-        second_image, (shape(256, 2, 128, dtype=BF16), shape(SIDES, PT)), name="second_image"
+        second_image, (shape(2 * GRP, 2, 128), shape(SIDES, PT)), name="second_image"
     )(part, dir1, w)
-    grams = lax.all_to_all(grams, ALL, 0, 0, tiled=True)
+    grams = lax.all_to_all(grams, GROUP_LAST, 0, 0, tiled=True)
     return call(finish, (shape(SIDES, PT), shape(SIDES, PT)), name="finish")(
         grams, gram1, sol1, res1, dir1, img1
     )

time: 125 us -> 123 us (0.984)
  blocking collectives: 67.4 us -> 64.4 us
  waiting for transfers between devices: 6.18 us -> 7.53 us
    all_to_all x2, blocking collectives: 29.4 us -> 25.6 us  [the longest x1 13.2 us: per_device(): grams = lax.all_to_all(grams, GROUP_LAST, 0, 0, tiled=True)]
    ppermute x2, waiting for transfers between devices: 0.01 us -> 1.35 us  [swap_cores(): return lax.ppermute(array, 'core', ((0, 1), (1, 0)))]
  transfers between devices with their start and end apart: 7 -> 7, of which waited for: 2 -> 3; matrix products, arithmetic and copies ran while one was open for 1% -> 1% of each run, Pallas kernels for 6% -> 6%
where the time goes in v5:
time: 123 us
  blocking collectives  64.4 us (52%)
  Pallas kernels  25.6 us (21%)
  starting transfers between devices  23.5 us (19%)
  waiting for transfers between devices  7.53 us (6%)
    all_to_all x2, blocking collectives, per_device(): part = lax.all_to_all(part, 'z', 0, 0, tiled=True)  23.8 us
    all_to_all x1, blocking collectives, per_device(): own_i = lax.all_to_all(message, GROUP_C, 0, 0, tiled=True)  15 us
    all_to_all x1, blocking collectives, per_device(): grams = lax.all_to_all(grams, GROUP_LAST, 0, 0, tiled=True)  13.2 us
    all_to_all x1, blocking collectives, per_device(): along_z = lax.all_to_all(along_z, 'z', 0, 0, tiled=True)  12.5 us
    ppermute x4, starting transfers between devices, swap_along_z(): return lax.ppermute(array, 'z', [(i, i ^ k) for i in range(DEPTH)])  9.65 us
    all_to_all x1, starting transfers between devices, per_device(): own_c = lax.all_to_all(msg_c, GROUP_C, 0, 0, tiled=True)  7.6 us
    pallas_call x1, Pallas kernels, per_device(): call(second_half, (shape(DEPTH, SIDES, PT), *half_tile), in_specs=[in_sme...  7.3 us
    pallas_call x1, Pallas kernels, per_device(): call(first_half, (shape(SIDES, ROWS), shape(AUG, ROWS, dtype=BF16), *half...  7.07 us
  transfers between devices with their start and end apart: 7, of which 3 were waited for; matrix products, arithmetic and copies ran while one was open for 1% of the time, Pallas kernels for 6%

profile of v5, /device:TPU:1, one launch (start us, length us, event | category | flops | bytes accessed | tf_op | source)
XLA Modules:
  0.0 122.6 jit_solution(11687411724818180558)
XLA Ops:
  0.6 2.6 %prepare.1 = (bf16[16,96,256]{2,1,0:T(8,128)(2,1)}, bf16[16,256]{1,0:T(8,128)(2,1)}, f32[16,256]{1,0:T(8,128)}, f32[1,256]{1,0:T(1,128)}) custom-call(bf16[64,256]{1,0:T(8,128)(2,1)} %emb_in.1, f32[1,256]{1,0:T(1,128)} %bitcast.4, s32[1,256]{1,0:T(1,128)} %bitcast.5, s32[1,256]{1,0:T(1,128)} %bitcast.6, f32[15,256]{1,0:T(8,128)} %probes_in.1), custom_call_target="tpu_custom_call" | custom-call | tf_op jit(solution)/shard_map/prepare/pallas_call | solution.py:290
  3.2 0.0 copy-start
  3.3 0.0 copy-start.2
  3.3 7.6 %all-to-all-start = ((bf16[16,96,256]{2,1,0:T(8,128)(2,1)}), bf16[16,96,256]{2,1,0:T(8,128)(2,1)S(1)}, u32[]{:S(2)}, u32[]{:S(2)}) async-start(bf16[16,96,256]{2,1,0:T(8,128)(2,1)} %get-tuple-element.40), calls=%async_computation | async-start | bytes 1572864 | tf_op jit(solution)/shard_map/all_to_all | solution.py:310
  10.9 0.0 copy-start.1
  10.9 1.7 %collective-permute-start = (bf16[64,256]{1,0:T(8,128)(2,1)}, bf16[64,256]{1,0:T(8,128)(2,1)S(1)}, u32[]{:S(2)}, u32[]{:S(2)}) collective-permute-start(bf16[64,256]{1,0:T(8,128)(2,1)} %emb_in.1), channel_id=1, source_target_pairs={{0,4},{4,0},{8,12},{12,8},{16,20},{20,16},{24,28},{28,24},{1,5},{5... | collective-permute-start | bytes 98312 | tf_op jit(solution)/shard_map/ppermute | solution.py:280
  12.6 0.8 constant_dynamic-update-slice_fusion.1
  13.4 0.7 collective-permute-done
  14.1 5.8 %collective-permute-start.3 = (bf16[64,512]{1,0:T(8,128)(2,1)S(1)}, bf16[64,512]{1,0:T(8,128)(2,1)S(1)}, u32[]{:S(2)}, u32[]{:S(2)}) collective-permute-start(bf16[64,512]{1,0:T(8,128)(2,1)S(1)} %constant_dynamic-update-slice_fusion.more_0_), channel_id=1, source_target_pairs={{0,24},{4,28},{8,16},{12,20},{16,8},{20,12},{24,0},{28,4},{1,25},{... | collective-permute-start | bytes 196616 | tf_op jit(solution)/shard_map/ppermute | solution.py:280
  20.0 0.9 collective-permute-start.2
  20.9 1.2 collective-permute-start.1
  22.1 0.0 collective-permute-done.3.more_3_
  22.1 5.4 %collective-permute-done.2.more_2_ = bf16[64,512]{1,0:T(8,128)(2,1)S(1)} collective-permute-done((bf16[64,512]{1,0:T(8,128)(2,1)S(1)}, bf16[64,512]{1,0:T(8,128)(2,1)S(1)}, u32[]{:S(2)}, u32[]{:S(2)}) %collective-permute-start.2) | collective-permute-done | bytes 65568 | tf_op jit(solution)/shard_map/ppermute | solution.py:280
  27.5 0.0 collective-permute-done.1.more_1_
  27.5 0.0 all-to-all-done.c_ref.own_s
  27.5 3.3 %collective-permute-start.4 = (bf16[16,96,256]{2,1,0:T(8,128)(2,1)S(1)}, bf16[16,96,256]{2,1,0:T(8,128)(2,1)S(1)}, u32[]{:S(2)}, u32[]{:S(2)}) collective-permute-start(bf16[16,96,256]{2,1,0:T(8,128)(2,1)S(1)} %all-to-all-done.c_ref.own_s), channel_id=1, source_target_pairs={{0,32},{32,0},{1,33},{33,1},{2,34},{34,2},{3,35},{35,3},{4,36},{36... | collective-permute-start | bytes 2359304 | tf_op jit(solution)/shard_map/ppermute | solution.py:284
  30.9 7.1 %first_half.1 = (f32[16,2048]{1,0:T(8,128)S(1)}, bf16[80,2048]{1,0:T(8,128)(2,1)S(1)}, bf16[512,2048]{1,0:T(8,128)(2,1)S(1)}, bf16[512,2048]{1,0:T(8,128)(2,1)S(...) custom-call(bf16[16,96,256]{2,1,0:T(8,128)(2,1)S(1)} %all-to-all-don, ...), custom_call_target="tpu_custom_call" | custom-call | tf_op jit(solution)/shard_map/first_half/pallas_call | solution.py:321
  37.9 0.0 collective-permute-done.4.c_ref.other_s
  37.9 7.3 %second_half.1 = (f32[8,16,256]{2,1,0:T(8,128)S(1)}, bf16[512,2048]{1,0:T(8,128)(2,1)S(1)}, bf16[512,2048]{1,0:T(8,128)(2,1)S(1)}, bf16[512,2048]{1,0:T(8,128)(2...) custom-call(s32[1]{0:T(128)} %bitcast.place, ...), custom_call_target="tpu_custom_call" | custom-call | tf_op jit(solution)/shard_map/second_half/pallas_call | solution.py:329
  45.2 13.0 %all_to_all.30.parts = f32[8,16,256]{2,1,0:T(8,128)S(1)} all-to-all(f32[8,16,256]{2,1,0:T(8,128)S(1)} %get-tuple-element.48), channel_id=1, replica_groups=mesh['y'=4,'core'=2,'z'=8,'x'=4] {'z'}, dimensions={0} | all-to-all | bytes 262144 | tf_op jit(solution)/shard_map/all_to_all | solution.py:338
  58.2 0.0 copy-done
  58.2 0.0 copy-done.2
  58.2 0.2 first_image.1
  58.5 15.0 %all_to_all.31.own.own_i = f32[16,24,256]{2,1,0:T(8,128)S(1)} all-to-all(f32[16,24,256]{2,1,0:T(8,128)S(1)} %get-tuple-element.51), channel_id=1, replica_groups=mesh['y'=4,'core'=2,'z'=8,'x'=4] {'y','x'}, dimensions={0} | all-to-all | bytes 786432 | tf_op jit(solution)/shard_map/all_to_all | solution.py:345
  73.4 2.9 %collective-permute-start.5 = (f32[16,24,256]{2,1,0:T(8,128)S(1)}, f32[16,24,256]{2,1,0:T(8,128)S(1)}, u32[]{:S(2)}, u32[]{:S(2)}) collective-permute-start(f32[16,24,256]{2,1,0:T(8,128)S(1)} %all_to_all.31.own.own_i), channel_id=1, source_target_pairs={{0,32},{32,0},{1,33},{33,1},{2,34},{34,2},{3,35},{35,3},{4,36},{36... | collective-permute-start | bytes 1179656 | tf_op jit(solution)/shard_map/ppermute | solution.py:284
  76.4 1.3 %collective-permute-done.5.other.other_i = f32[16,24,256]{2,1,0:T(8,128)S(1)} collective-permute-done((f32[16,24,256]{2,1,0:T(8,128)S(1)}, f32[16,24,256]{2,1,0:T(8,128)S(1)}, u32[]{:S(2)}, u32[]{:S(2)}) %collective-permute-start.5) | collective-permute-done | bytes 393248 | tf_op jit(solution)/shard_map/ppermute | solution.py:284
  77.8 12.5 %all_to_all.32.along_z = bf16[8,48,256]{2,1,0:T(8,128)(2,1)S(1)} all-to-all(bf16[8,48,256]{2,1,0:T(8,128)(2,1)S(1)} %gram_sum.1), channel_id=1, replica_groups=mesh['y'=4,'core'=2,'z'=8,'x'=4] {'z'}, dimensions={0} | all-to-all | bytes 393216 | tf_op jit(solution)/shard_map/all_to_all | solution.py:357
  90.2 6.9 %second_apply.1 = (f32[8,24,256]{2,1,0:T(8,128)S(1)}, f32[16,256]{1,0:T(8,128)S(1)}, f32[16,256]{1,0:T(8,128)S(1)}, f32[16,256]{1,0:T(8,128)S(1)}, f32[16,16]{1,0:T(8,128)S(1)}) custom-call(s32[1]{0:T(128)} %bitcast.place, bf16[8,48,256]{2,1,0:T(8,128)(2,1)S(1)} %all_to_all.32.along_z, f32[16,24,256]{2,1,0:T(8,128)S(1)} %all_to_all.31.own.own_i, ...), custom_call_target="tpu_custom_call" | custom-call | tf_op jit(solution)/shard_map/second_apply/pallas_call | solution.py:361
  97.1 10.8 %all_to_all.33.parts = f32[8,24,256]{2,1,0:T(8,128)S(1)} all-to-all(f32[8,24,256]{2,1,0:T(8,128)S(1)} %get-tuple-element.71), channel_id=1, replica_groups=mesh['y'=4,'core'=2,'z'=8,'x'=4] {'z'}, dimensions={0} | all-to-all | bytes 393216 | tf_op jit(solution)/shard_map/all_to_all | solution.py:377
  107.9 0.2 second_image.1
  108.1 13.2 %all_to_all.34.grams = f32[32,2,128]{2,1,0:T(2,128)S(1)} all-to-all(f32[32,2,128]{2,1,0:T(2,128)S(1)} %get-tuple-element.73), channel_id=1, replica_groups=mesh['y'=4,'core'=2,'z'=8,'x'=4] {'y','core','x'}, dimensions={0} | all-to-all | bytes 65536 | tf_op jit(solution)/shard_map/all_to_all | solution.py:382
  121.3 1.3 %finish.1 = (f32[16,256]{1,0:T(8,128)}, f32[16,256]{1,0:T(8,128)}) custom-call(f32[32,2,128]{2,1,0:T(2,128)S(1)} %all_to_all.34.grams, f32[16,16]{1,0:T(8,128)S(1)} %get-tuple-element.74.gram1, f32[16,256]{1,0:T(8,128)S(1)} %get-tuple-element.75.sol1, f32[16,256]{1,0:T(8,128)S(1)} %get-tuple-element.76.res1, f32[16,256]{1,0:T(8,128)S(1)} %get-tuple-element.72.base.dir1, ...), custom_call_target="tpu_custom_call" | custom-call | tf_op jit(solution)/shard_map/finish/pallas_call | solution.py:383
  (3 shorter events, 0.0 us)
Async XLA Ops:
  3.2 55.0 %copy-start = (f32[16,256]{1,0:T(8,128)S(1)}, f32[16,256]{1,0:T(8,128)}, u32[]{:S(2)}) copy-start(f32[16,256]{1,0:T(8,128)} %get-tuple-element.49.base.more_0_) | copy-start | bytes 49156
  3.3 55.0 %copy-start.2 = (f32[1,256]{1,0:T(1,128)S(1)}, f32[1,256]{1,0:T(1,128)}, u32[]{:S(2)}) copy-start(f32[1,256]{1,0:T(1,128)} %get-tuple-element.50.w) | copy-start | bytes 3076
  3.3 24.2 %all-to-all-start = ((bf16[16,96,256]{2,1,0:T(8,128)(2,1)}), bf16[16,96,256]{2,1,0:T(8,128)(2,1)S(1)}, u32[]{:S(2)}, u32[]{:S(2)}) async-start(bf16[16,96,256]{2,1,0:T(8,128)(2,1)} %get-tuple-element.40), calls=%async_computation | async-start | bytes 1572864 | tf_op jit(solution)/shard_map/all_to_all | solution.py:310
  10.9 66.9 %copy-start.1 = (bf16[16,256]{1,0:T(8,128)(2,1)S(1)}, bf16[16,256]{1,0:T(8,128)(2,1)}, u32[]{:S(2)}) copy-start(bf16[16,256]{1,0:T(8,128)(2,1)} %get-tuple-element.52.scaled) | copy-start | bytes 24580
  10.9 3.2 %collective-permute-start = (bf16[64,256]{1,0:T(8,128)(2,1)}, bf16[64,256]{1,0:T(8,128)(2,1)S(1)}, u32[]{:S(2)}, u32[]{:S(2)}) collective-permute-start(bf16[64,256]{1,0:T(8,128)(2,1)} %emb_in.1), channel_id=1, source_target_pairs={{0,4},{4,0},{8,12},{12,8},{16,20},{20,16},{24,28},{28,24},{1,5},{5... | collective-permute-start | bytes 98312 | tf_op jit(solution)/shard_map/ppermute | solution.py:280
  14.1 7.9 %collective-permute-start.3 = (bf16[64,512]{1,0:T(8,128)(2,1)S(1)}, bf16[64,512]{1,0:T(8,128)(2,1)S(1)}, u32[]{:S(2)}, u32[]{:S(2)}) collective-permute-start(bf16[64,512]{1,0:T(8,128)(2,1)S(1)} %constant_dynamic-update-slice_fusion.more_0_), channel_id=1, source_target_pairs={{0,24},{4,28},{8,16},{12,20},{16,8},{20,12},{24,0},{28,4},{1,25},{... | collective-permute-start | bytes 196616 | tf_op jit(solution)/shard_map/ppermute | solution.py:280
  20.0 7.5 %collective-permute-start.2 = (bf16[64,512]{1,0:T(8,128)(2,1)S(1)}, bf16[64,512]{1,0:T(8,128)(2,1)S(1)}, u32[]{:S(2)}, u32[]{:S(2)}) collective-permute-start(bf16[64,512]{1,0:T(8,128)(2,1)S(1)} %constant_dynamic-update-slice_fusion.more_0_), channel_id=1, source_target_pairs={{0,16},{4,20},{8,24},{12,28},{16,0},{20,4},{24,8},{28,12},{1,17},{... | collective-permute-start | bytes 196616 | tf_op jit(solution)/shard_map/ppermute | solution.py:280
  20.9 6.6 %collective-permute-start.1 = (bf16[64,512]{1,0:T(8,128)(2,1)S(1)}, bf16[64,512]{1,0:T(8,128)(2,1)S(1)}, u32[]{:S(2)}, u32[]{:S(2)}) collective-permute-start(bf16[64,512]{1,0:T(8,128)(2,1)S(1)} %constant_dynamic-update-slice_fusion.more_0_), channel_id=1, source_target_pairs={{0,8},{4,12},{8,0},{12,4},{16,24},{20,28},{24,16},{28,20},{1,9},{5... | collective-permute-start | bytes 196616 | tf_op jit(solution)/shard_map/ppermute | solution.py:280
  27.5 10.4 %collective-permute-start.4 = (bf16[16,96,256]{2,1,0:T(8,128)(2,1)S(1)}, bf16[16,96,256]{2,1,0:T(8,128)(2,1)S(1)}, u32[]{:S(2)}, u32[]{:S(2)}) collective-permute-start(bf16[16,96,256]{2,1,0:T(8,128)(2,1)S(1)} %all-to-all-done.c_ref.own_s), channel_id=1, source_target_pairs={{0,32},{32,0},{1,33},{33,1},{2,34},{34,2},{3,35},{35,3},{4,36},{36... | collective-permute-start | bytes 2359304 | tf_op jit(solution)/shard_map/ppermute | solution.py:284
  73.4 4.3 %collective-permute-start.5 = (f32[16,24,256]{2,1,0:T(8,128)S(1)}, f32[16,24,256]{2,1,0:T(8,128)S(1)}, u32[]{:S(2)}, u32[]{:S(2)}) collective-permute-start(f32[16,24,256]{2,1,0:T(8,128)S(1)} %all_to_all.31.own.own_i), channel_id=1, source_target_pairs={{0,32},{32,0},{1,33},{33,1},{2,34},{34,2},{3,35},{35,3},{4,36},{36... | collective-permute-start | bytes 1179656 | tf_op jit(solution)/shard_map/ppermute | solution.py:284

commit v6 on v5

--- a/solution.py
+++ b/solution.py
@@ -18,6 +18,7 @@
 GRP = 16
 DEPTH = 8
 PAIRS = DEPTH // 2
+ORDER = (0, 1, 6, 7, 2, 3, 4, 5)
 HALF = GRP * PT
 COLS = 2 * HALF
 ROWS = DEPTH * PT
@@ -152,7 +153,7 @@
     total = half_apply(c_ref, right, more[: PIECES // 2], *more[PIECES // 2 :])
     total = total + before[...]
     for k in range(DEPTH):
-        out[lax.bitwise_xor(place[0], k)] = total[:, k * PT : (k + 1) * PT]
+        out[lax.bitwise_xor(place[0], ORDER[k])] = total[:, k * PT : (k + 1) * PT]
 
 
 def unpack(total, n):
@@ -227,14 +228,14 @@
         total += jnp.dot(vec[j], kernel, preferred_element_type=F32)
     weighted = []
     for k in range(DEPTH):
-        both = along_z[lax.bitwise_xor(place[0], k), : 2 * SIDES, :].astype(F32)
+        both = along_z[lax.bitwise_xor(place[0], ORDER[k]), : 2 * SIDES, :].astype(F32)
         weighted.append(hdot(coef, both, ((0,), (0,))))
     gram = hdot(d1, d1, ((1,), (1,)))
     gram = gram + hdot(jnp.concatenate(weighted, axis=1), total, ((1,), (1,)))
     gram = jnp.concatenate([gram[:8], gram[8:], jnp.zeros((8, PT - 32), F32)], axis=1)
     for k in range(DEPTH):
         part = total[:, k * PT : (k + 1) * PT]
-        out[lax.bitwise_xor(place[0], k)] = jnp.concatenate([part, gram], axis=0)
+        out[lax.bitwise_xor(place[0], ORDER[k])] = jnp.concatenate([part, gram], axis=0)
 
 
 def second_image(parts, base, w, out, image):
@@ -309,7 +310,7 @@
     )(embeddings, latent[None, :], list_of[None, :], rank_of[None, :], probes)
     own_c = lax.all_to_all(msg_c, GROUP_C, 0, 0, tiled=True)
     pair = jnp.concatenate([embeddings, swap_along_z(embeddings, 1)], axis=1)
-    all_r = [pair] + [swap_along_z(pair, k) for k in range(2, DEPTH, 2)]
+    all_r = [pair] + [swap_along_z(pair, k) for k in ORDER[2::2]]
     own_c, all_r = lax.optimization_barrier((own_c, all_r))
     other_c = swap_cores(own_c)
 

time: 123 us -> 122 us (level)
  blocking collectives: 64.4 us -> 62.9 us
    all_to_all x2, blocking collectives: 23.8 us -> 22.4 us  [per_device(): part = lax.all_to_all(part, 'z', 0, 0, tiled=True)]
  transfers between devices with their start and end apart: 7 -> 7, of which waited for: 3 -> 5; matrix products, arithmetic and copies ran while one was open for 1% -> 1% of each run, Pallas kernels for 6% -> 6%
where the time goes in v6:
time: 122 us; the launch traced here: 121 us
  blocking collectives  62.9 us (52%)
  Pallas kernels  25.5 us (21%)
  starting transfers between devices  24 us (20%)
  waiting for transfers between devices  7.4 us (6%)
    all_to_all x2, blocking collectives, per_device(): part = lax.all_to_all(part, 'z', 0, 0, tiled=True)  22.4 us
    all_to_all x1, blocking collectives, per_device(): own_i = lax.all_to_all(message, GROUP_C, 0, 0, tiled=True)  14.7 us
    all_to_all x1, blocking collectives, per_device(): grams = lax.all_to_all(grams, GROUP_LAST, 0, 0, tiled=True)  13.3 us
    all_to_all x1, blocking collectives, per_device(): along_z = lax.all_to_all(along_z, 'z', 0, 0, tiled=True)  12.5 us
    ppermute x4, starting transfers between devices, swap_along_z(): return lax.ppermute(array, 'z', [(i, i ^ k) for i in range(DEPTH)])  9.65 us
    all_to_all x1, starting transfers between devices, per_device(): own_c = lax.all_to_all(msg_c, GROUP_C, 0, 0, tiled=True)  7.6 us
    pallas_call x1, Pallas kernels, per_device(): call(second_half, (shape(DEPTH, SIDES, PT), *half_tile), in_specs=[in_sme...  7.3 us
    pallas_call x1, Pallas kernels, per_device(): call(first_half, (shape(SIDES, ROWS), shape(AUG, ROWS, dtype=BF16), *half...  7.07 us
  transfers between devices with their start and end apart: 7, of which 5 were waited for; matrix products, arithmetic and copies ran while one was open for 1% of the time, Pallas kernels for 6%

profile of v6, /device:TPU:1, one launch (start us, length us, event | category | flops | bytes accessed | tf_op | source)
XLA Modules:
  0.0 121.3 jit_solution(10486155452497852579)
XLA Ops:
  0.6 2.6 %prepare.1 = (bf16[16,96,256]{2,1,0:T(8,128)(2,1)}, bf16[16,256]{1,0:T(8,128)(2,1)}, f32[16,256]{1,0:T(8,128)}, f32[1,256]{1,0:T(1,128)}) custom-call(bf16[64,256]{1,0:T(8,128)(2,1)} %emb_in.1, f32[1,256]{1,0:T(1,128)} %bitcast.4, s32[1,256]{1,0:T(1,128)} %bitcast.5, s32[1,256]{1,0:T(1,128)} %bitcast.6, f32[15,256]{1,0:T(8,128)} %probes_in.1), custom_call_target="tpu_custom_call" | custom-call | tf_op jit(solution)/shard_map/prepare/pallas_call | solution.py:291
  3.2 0.0 copy-start
  3.3 0.0 copy-start.2
  3.3 7.6 %all-to-all-start = ((bf16[16,96,256]{2,1,0:T(8,128)(2,1)}), bf16[16,96,256]{2,1,0:T(8,128)(2,1)S(1)}, u32[]{:S(2)}, u32[]{:S(2)}) async-start(bf16[16,96,256]{2,1,0:T(8,128)(2,1)} %get-tuple-element.40), calls=%async_computation | async-start | bytes 1572864 | tf_op jit(solution)/shard_map/all_to_all | solution.py:311
  10.9 0.0 copy-start.1
  10.9 1.7 %collective-permute-start = (bf16[64,256]{1,0:T(8,128)(2,1)}, bf16[64,256]{1,0:T(8,128)(2,1)S(1)}, u32[]{:S(2)}, u32[]{:S(2)}) collective-permute-start(bf16[64,256]{1,0:T(8,128)(2,1)} %emb_in.1), channel_id=1, source_target_pairs={{0,4},{4,0},{8,12},{12,8},{16,20},{20,16},{24,28},{28,24},{1,5},{5... | collective-permute-start | bytes 98312 | tf_op jit(solution)/shard_map/ppermute | solution.py:281
  12.6 0.8 constant_dynamic-update-slice_fusion.1
  13.4 0.7 collective-permute-done
  14.1 6.7 %collective-permute-start.3 = (bf16[64,512]{1,0:T(8,128)(2,1)S(1)}, bf16[64,512]{1,0:T(8,128)(2,1)S(1)}, u32[]{:S(2)}, u32[]{:S(2)}) collective-permute-start(bf16[64,512]{1,0:T(8,128)(2,1)S(1)} %constant_dynamic-update-slice_fusion.more_0_), channel_id=1, source_target_pairs={{0,16},{4,20},{8,24},{12,28},{16,0},{20,4},{24,8},{28,12},{1,17},{... | collective-permute-start | bytes 196616 | tf_op jit(solution)/shard_map/ppermute | solution.py:281
  20.9 1.2 collective-permute-start.2
  22.1 0.0 collective-permute-start.1
  22.1 0.8 collective-permute-done.3.more_3_
  22.8 4.2 %collective-permute-done.2.more_2_ = bf16[64,512]{1,0:T(8,128)(2,1)S(1)} collective-permute-done((bf16[64,512]{1,0:T(8,128)(2,1)S(1)}, bf16[64,512]{1,0:T(8,128)(2,1)S(1)}, u32[]{:S(2)}, u32[]{:S(2)}) %collective-permute-start.2) | collective-permute-done | bytes 65568 | tf_op jit(solution)/shard_map/ppermute | solution.py:281
  27.0 0.4 collective-permute-done.1.more_1_
  27.4 0.0 all-to-all-done.c_ref.own_s
  27.4 3.8 %collective-permute-start.4 = (bf16[16,96,256]{2,1,0:T(8,128)(2,1)S(1)}, bf16[16,96,256]{2,1,0:T(8,128)(2,1)S(1)}, u32[]{:S(2)}, u32[]{:S(2)}) collective-permute-start(bf16[16,96,256]{2,1,0:T(8,128)(2,1)S(1)} %all-to-all-done.c_ref.own_s), channel_id=1, source_target_pairs={{0,32},{32,0},{1,33},{33,1},{2,34},{34,2},{3,35},{35,3},{4,36},{36... | collective-permute-start | bytes 2359304 | tf_op jit(solution)/shard_map/ppermute | solution.py:285
  31.2 7.1 %first_half.1 = (f32[16,2048]{1,0:T(8,128)S(1)}, bf16[80,2048]{1,0:T(8,128)(2,1)S(1)}, bf16[512,2048]{1,0:T(8,128)(2,1)S(1)}, bf16[512,2048]{1,0:T(8,128)(2,1)S(...) custom-call(bf16[16,96,256]{2,1,0:T(8,128)(2,1)S(1)} %all-to-all-don, ...), custom_call_target="tpu_custom_call" | custom-call | tf_op jit(solution)/shard_map/first_half/pallas_call | solution.py:322
  38.3 0.0 collective-permute-done.4.c_ref.other_s
  38.3 7.3 %second_half.1 = (f32[8,16,256]{2,1,0:T(8,128)S(1)}, bf16[512,2048]{1,0:T(8,128)(2,1)S(1)}, bf16[512,2048]{1,0:T(8,128)(2,1)S(1)}, bf16[512,2048]{1,0:T(8,128)(2...) custom-call(s32[1]{0:T(128)} %bitcast.place, ...), custom_call_target="tpu_custom_call" | custom-call | tf_op jit(solution)/shard_map/second_half/pallas_call | solution.py:330
  45.6 11.6 %all_to_all.30.parts = f32[8,16,256]{2,1,0:T(8,128)S(1)} all-to-all(f32[8,16,256]{2,1,0:T(8,128)S(1)} %get-tuple-element.48), channel_id=1, replica_groups=mesh['y'=4,'core'=2,'z'=8,'x'=4] {'z'}, dimensions={0} | all-to-all | bytes 262144 | tf_op jit(solution)/shard_map/all_to_all | solution.py:339
  57.2 0.0 copy-done
  57.2 0.2 first_image.1
  57.4 14.7 %all_to_all.31.own.own_i = f32[16,24,256]{2,1,0:T(8,128)S(1)} all-to-all(f32[16,24,256]{2,1,0:T(8,128)S(1)} %get-tuple-element.51), channel_id=1, replica_groups=mesh['y'=4,'core'=2,'z'=8,'x'=4] {'y','x'}, dimensions={0} | all-to-all | bytes 786432 | tf_op jit(solution)/shard_map/all_to_all | solution.py:346
  72.2 2.9 %collective-permute-start.5 = (f32[16,24,256]{2,1,0:T(8,128)S(1)}, f32[16,24,256]{2,1,0:T(8,128)S(1)}, u32[]{:S(2)}, u32[]{:S(2)}) collective-permute-start(f32[16,24,256]{2,1,0:T(8,128)S(1)} %all_to_all.31.own.own_i), channel_id=1, source_target_pairs={{0,32},{32,0},{1,33},{33,1},{2,34},{34,2},{3,35},{35,3},{4,36},{36... | collective-permute-start | bytes 1179656 | tf_op jit(solution)/shard_map/ppermute | solution.py:285
  75.1 1.3 %collective-permute-done.5.other.other_i = f32[16,24,256]{2,1,0:T(8,128)S(1)} collective-permute-done((f32[16,24,256]{2,1,0:T(8,128)S(1)}, f32[16,24,256]{2,1,0:T(8,128)S(1)}, u32[]{:S(2)}, u32[]{:S(2)}) %collective-permute-start.5) | collective-permute-done | bytes 393248 | tf_op jit(solution)/shard_map/ppermute | solution.py:285
  76.4 0.0 copy-done.1
  76.5 12.5 %all_to_all.32.along_z = bf16[8,48,256]{2,1,0:T(8,128)(2,1)S(1)} all-to-all(bf16[8,48,256]{2,1,0:T(8,128)(2,1)S(1)} %gram_sum.1), channel_id=1, replica_groups=mesh['y'=4,'core'=2,'z'=8,'x'=4] {'z'}, dimensions={0} | all-to-all | bytes 393216 | tf_op jit(solution)/shard_map/all_to_all | solution.py:358
  88.9 6.8 %second_apply.1 = (f32[8,24,256]{2,1,0:T(8,128)S(1)}, f32[16,256]{1,0:T(8,128)S(1)}, f32[16,256]{1,0:T(8,128)S(1)}, f32[16,256]{1,0:T(8,128)S(1)}, f32[16,16]{1,0:T(8,128)S(1)}) custom-call(s32[1]{0:T(128)} %bitcast.place, bf16[8,48,256]{2,1,0:T(8,128)(2,1)S(1)} %all_to_all.32.along_z, f32[16,24,256]{2,1,0:T(8,128)S(1)} %all_to_all.31.own.own_i, ...), custom_call_target="tpu_custom_call" | custom-call | tf_op jit(solution)/shard_map/second_apply/pallas_call | solution.py:362
  95.8 10.8 %all_to_all.33.parts = f32[8,24,256]{2,1,0:T(8,128)S(1)} all-to-all(f32[8,24,256]{2,1,0:T(8,128)S(1)} %get-tuple-element.71), channel_id=1, replica_groups=mesh['y'=4,'core'=2,'z'=8,'x'=4] {'z'}, dimensions={0} | all-to-all | bytes 393216 | tf_op jit(solution)/shard_map/all_to_all | solution.py:378
  106.5 0.2 second_image.1
  106.7 13.3 %all_to_all.34.grams = f32[32,2,128]{2,1,0:T(2,128)S(1)} all-to-all(f32[32,2,128]{2,1,0:T(2,128)S(1)} %get-tuple-element.73), channel_id=1, replica_groups=mesh['y'=4,'core'=2,'z'=8,'x'=4] {'y','core','x'}, dimensions={0} | all-to-all | bytes 65536 | tf_op jit(solution)/shard_map/all_to_all | solution.py:383
  120.0 1.3 %finish.1 = (f32[16,256]{1,0:T(8,128)}, f32[16,256]{1,0:T(8,128)}) custom-call(f32[32,2,128]{2,1,0:T(2,128)S(1)} %all_to_all.34.grams, f32[16,16]{1,0:T(8,128)S(1)} %get-tuple-element.74.gram1, f32[16,256]{1,0:T(8,128)S(1)} %get-tuple-element.75.sol1, f32[16,256]{1,0:T(8,128)S(1)} %get-tuple-element.76.res1, f32[16,256]{1,0:T(8,128)S(1)} %get-tuple-element.72.base.dir1, ...), custom_call_target="tpu_custom_call" | custom-call | tf_op jit(solution)/shard_map/finish/pallas_call | solution.py:384
  (3 shorter events, 0.0 us)
Async XLA Ops:
  3.2 53.9 %copy-start = (f32[16,256]{1,0:T(8,128)S(1)}, f32[16,256]{1,0:T(8,128)}, u32[]{:S(2)}) copy-start(f32[16,256]{1,0:T(8,128)} %get-tuple-element.49.base.more_0_) | copy-start | bytes 49156
  3.3 53.9 %copy-start.2 = (f32[1,256]{1,0:T(1,128)S(1)}, f32[1,256]{1,0:T(1,128)}, u32[]{:S(2)}) copy-start(f32[1,256]{1,0:T(1,128)} %get-tuple-element.50.w) | copy-start | bytes 3076
  3.3 24.1 %all-to-all-start = ((bf16[16,96,256]{2,1,0:T(8,128)(2,1)}), bf16[16,96,256]{2,1,0:T(8,128)(2,1)S(1)}, u32[]{:S(2)}, u32[]{:S(2)}) async-start(bf16[16,96,256]{2,1,0:T(8,128)(2,1)} %get-tuple-element.40), calls=%async_computation | async-start | bytes 1572864 | tf_op jit(solution)/shard_map/all_to_all | solution.py:311
  10.9 65.6 %copy-start.1 = (bf16[16,256]{1,0:T(8,128)(2,1)S(1)}, bf16[16,256]{1,0:T(8,128)(2,1)}, u32[]{:S(2)}) copy-start(bf16[16,256]{1,0:T(8,128)(2,1)} %get-tuple-element.52.scaled) | copy-start | bytes 24580
  10.9 3.2 %collective-permute-start = (bf16[64,256]{1,0:T(8,128)(2,1)}, bf16[64,256]{1,0:T(8,128)(2,1)S(1)}, u32[]{:S(2)}, u32[]{:S(2)}) collective-permute-start(bf16[64,256]{1,0:T(8,128)(2,1)} %emb_in.1), channel_id=1, source_target_pairs={{0,4},{4,0},{8,12},{12,8},{16,20},{20,16},{24,28},{28,24},{1,5},{5... | collective-permute-start | bytes 98312 | tf_op jit(solution)/shard_map/ppermute | solution.py:281
  14.1 8.7 %collective-permute-start.3 = (bf16[64,512]{1,0:T(8,128)(2,1)S(1)}, bf16[64,512]{1,0:T(8,128)(2,1)S(1)}, u32[]{:S(2)}, u32[]{:S(2)}) collective-permute-start(bf16[64,512]{1,0:T(8,128)(2,1)S(1)} %constant_dynamic-update-slice_fusion.more_0_), channel_id=1, source_target_pairs={{0,16},{4,20},{8,24},{12,28},{16,0},{20,4},{24,8},{28,12},{1,17},{... | collective-permute-start | bytes 196616 | tf_op jit(solution)/shard_map/ppermute | solution.py:281
  20.9 6.2 %collective-permute-start.2 = (bf16[64,512]{1,0:T(8,128)(2,1)S(1)}, bf16[64,512]{1,0:T(8,128)(2,1)S(1)}, u32[]{:S(2)}, u32[]{:S(2)}) collective-permute-start(bf16[64,512]{1,0:T(8,128)(2,1)S(1)} %constant_dynamic-update-slice_fusion.more_0_), channel_id=1, source_target_pairs={{0,8},{4,12},{8,0},{12,4},{16,24},{20,28},{24,16},{28,20},{1,9},{5... | collective-permute-start | bytes 196616 | tf_op jit(solution)/shard_map/ppermute | solution.py:281
  22.1 5.3 %collective-permute-start.1 = (bf16[64,512]{1,0:T(8,128)(2,1)S(1)}, bf16[64,512]{1,0:T(8,128)(2,1)S(1)}, u32[]{:S(2)}, u32[]{:S(2)}) collective-permute-start(bf16[64,512]{1,0:T(8,128)(2,1)S(1)} %constant_dynamic-update-slice_fusion.more_0_), channel_id=1, source_target_pairs={{0,24},{4,28},{8,16},{12,20},{16,8},{20,12},{24,0},{28,4},{1,25},{... | collective-permute-start | bytes 196616 | tf_op jit(solution)/shard_map/ppermute | solution.py:281
  27.4 10.9 %collective-permute-start.4 = (bf16[16,96,256]{2,1,0:T(8,128)(2,1)S(1)}, bf16[16,96,256]{2,1,0:T(8,128)(2,1)S(1)}, u32[]{:S(2)}, u32[]{:S(2)}) collective-permute-start(bf16[16,96,256]{2,1,0:T(8,128)(2,1)S(1)} %all-to-all-done.c_ref.own_s), channel_id=1, source_target_pairs={{0,32},{32,0},{1,33},{33,1},{2,34},{34,2},{3,35},{35,3},{4,36},{36... | collective-permute-start | bytes 2359304 | tf_op jit(solution)/shard_map/ppermute | solution.py:285
  72.2 4.3 %collective-permute-start.5 = (f32[16,24,256]{2,1,0:T(8,128)S(1)}, f32[16,24,256]{2,1,0:T(8,128)S(1)}, u32[]{:S(2)}, u32[]{:S(2)}) collective-permute-start(f32[16,24,256]{2,1,0:T(8,128)S(1)} %all_to_all.31.own.own_i), channel_id=1, source_target_pairs={{0,32},{32,0},{1,33},{33,1},{2,34},{34,2},{3,35},{35,3},{4,36},{36... | collective-permute-start | bytes 1179656 | tf_op jit(solution)/shard_map/ppermute | solution.py:285

commit v7 on v6

--- a/solution.py
+++ b/solution.py
@@ -127,7 +127,7 @@
         rows = jnp.concatenate([points, ones, norm_rows(points), zeros], axis=0)
         left[at, :] = rows.astype(BF16).T
         vec[:, at] = c_ref[g, D : D + SIDES, :]
-    step = 256
+    step = 512
     total = jnp.zeros((SIDES, ROWS), F32)
     for j in range(HALF // step):
         at = slice(j * step, (j + 1) * step)
@@ -223,9 +223,9 @@
             both = jnp.concatenate([wr, i_ref[g]], axis=0)
             vec.append(hdot(coef, both, ((0,), (0,))).astype(BF16))
     total = jnp.zeros((SIDES, ROWS), F32)
-    for j in range(len(vec)):
-        kernel = tile[j * PT // PIECE][pl.ds(j * PT % PIECE, PT), :]
-        total += jnp.dot(vec[j], kernel, preferred_element_type=F32)
+    for j in range(PIECES):
+        scaled = jnp.concatenate(vec[j * PIECE // PT : (j + 1) * PIECE // PT], axis=1)
+        total += jnp.dot(scaled, tile[j][...], preferred_element_type=F32)
     weighted = []
     for k in range(DEPTH):
         both = along_z[lax.bitwise_xor(place[0], ORDER[k]), : 2 * SIDES, :].astype(F32)
@@ -325,6 +325,7 @@
         in_specs=[in_vmem] * (1 + PAIRS),
         out_specs=[in_vmem] * (2 + PIECES // 2),
         scratch_shapes=scratch,
+        vmem=14,
         name="first_half",
     )(own_c, *all_r)
     part, *more = call(
@@ -333,6 +334,7 @@
         in_specs=[in_smem] + [in_vmem] * 3,
         out_specs=[in_vmem] * (1 + PIECES // 2),
         scratch_shapes=scratch,
+        vmem=14,
         name="second_half",
     )(place, other_c, right, part)
     tile = tile + more

time: 122 us -> 121 us (level)
  no operation moved by 1% of the time
where the time goes in v7:
time: 121 us
  blocking collectives  62.8 us (52%)
  Pallas kernels  25.2 us (21%)
  starting transfers between devices  24 us (20%)
  waiting for transfers between devices  7.4 us (6%)
    all_to_all x2, blocking collectives, per_device(): part = lax.all_to_all(part, 'z', 0, 0, tiled=True)  22.4 us
    all_to_all x1, blocking collectives, per_device(): own_i = lax.all_to_all(message, GROUP_C, 0, 0, tiled=True)  14.7 us
    all_to_all x1, blocking collectives, per_device(): grams = lax.all_to_all(grams, GROUP_LAST, 0, 0, tiled=True)  13.2 us
    all_to_all x1, blocking collectives, per_device(): along_z = lax.all_to_all(along_z, 'z', 0, 0, tiled=True)  12.5 us
    ppermute x4, starting transfers between devices, swap_along_z(): return lax.ppermute(array, 'z', [(i, i ^ k) for i in range(DEPTH)])  9.65 us
    all_to_all x1, starting transfers between devices, per_device(): own_c = lax.all_to_all(msg_c, GROUP_C, 0, 0, tiled=True)  7.6 us
    pallas_call x1, Pallas kernels, per_device(): call(second_half, (shape(DEPTH, SIDES, PT), *half_tile), in_specs=[in_sme...  7.13 us
    pallas_call x1, Pallas kernels, per_device(): call(first_half, (shape(SIDES, ROWS), shape(AUG, ROWS, dtype=BF16), *half...  6.92 us
  transfers between devices with their start and end apart: 7, of which 5 were waited for; matrix products, arithmetic and copies ran while one was open for 1% of the time, Pallas kernels for 6%

profile of v7, /device:TPU:1, one launch (start us, length us, event | category | flops | bytes accessed | tf_op | source)
XLA Modules:
  0.0 121.0 jit_solution(14102254373958560236)
XLA Ops:
  0.6 2.6 %prepare.1 = (bf16[16,96,256]{2,1,0:T(8,128)(2,1)}, bf16[16,256]{1,0:T(8,128)(2,1)}, f32[16,256]{1,0:T(8,128)}, f32[1,256]{1,0:T(1,128)}) custom-call(bf16[64,256]{1,0:T(8,128)(2,1)} %emb_in.1, f32[1,256]{1,0:T(1,128)} %bitcast.4, s32[1,256]{1,0:T(1,128)} %bitcast.5, s32[1,256]{1,0:T(1,128)} %bitcast.6, f32[15,256]{1,0:T(8,128)} %probes_in.1), custom_call_target="tpu_custom_call" | custom-call | tf_op jit(solution)/shard_map/prepare/pallas_call | solution.py:291
  3.2 0.0 copy-start
  3.3 0.0 copy-start.2
  3.3 7.6 %all-to-all-start = ((bf16[16,96,256]{2,1,0:T(8,128)(2,1)}), bf16[16,96,256]{2,1,0:T(8,128)(2,1)S(1)}, u32[]{:S(2)}, u32[]{:S(2)}) async-start(bf16[16,96,256]{2,1,0:T(8,128)(2,1)} %get-tuple-element.40), calls=%async_computation | async-start | bytes 1572864 | tf_op jit(solution)/shard_map/all_to_all | solution.py:311
  10.9 0.0 copy-start.1
  10.9 1.7 %collective-permute-start = (bf16[64,256]{1,0:T(8,128)(2,1)}, bf16[64,256]{1,0:T(8,128)(2,1)S(1)}, u32[]{:S(2)}, u32[]{:S(2)}) collective-permute-start(bf16[64,256]{1,0:T(8,128)(2,1)} %emb_in.1), channel_id=1, source_target_pairs={{0,4},{4,0},{8,12},{12,8},{16,20},{20,16},{24,28},{28,24},{1,5},{5... | collective-permute-start | bytes 98312 | tf_op jit(solution)/shard_map/ppermute | solution.py:281
  12.6 0.8 constant_dynamic-update-slice_fusion.1
  13.4 0.7 collective-permute-done
  14.1 6.7 %collective-permute-start.3 = (bf16[64,512]{1,0:T(8,128)(2,1)S(1)}, bf16[64,512]{1,0:T(8,128)(2,1)S(1)}, u32[]{:S(2)}, u32[]{:S(2)}) collective-permute-start(bf16[64,512]{1,0:T(8,128)(2,1)S(1)} %constant_dynamic-update-slice_fusion.more_0_), channel_id=1, source_target_pairs={{0,16},{4,20},{8,24},{12,28},{16,0},{20,4},{24,8},{28,12},{1,17},{... | collective-permute-start | bytes 196616 | tf_op jit(solution)/shard_map/ppermute | solution.py:281
  20.9 1.2 collective-permute-start.2
  22.1 0.0 collective-permute-start.1
  22.1 0.8 collective-permute-done.3.more_3_
  22.8 4.2 %collective-permute-done.2.more_2_ = bf16[64,512]{1,0:T(8,128)(2,1)S(1)} collective-permute-done((bf16[64,512]{1,0:T(8,128)(2,1)S(1)}, bf16[64,512]{1,0:T(8,128)(2,1)S(1)}, u32[]{:S(2)}, u32[]{:S(2)}) %collective-permute-start.2) | collective-permute-done | bytes 65568 | tf_op jit(solution)/shard_map/ppermute | solution.py:281
  27.0 0.4 collective-permute-done.1.more_1_
  27.4 0.0 all-to-all-done.c_ref.own_s
  27.4 3.8 %collective-permute-start.4 = (bf16[16,96,256]{2,1,0:T(8,128)(2,1)S(1)}, bf16[16,96,256]{2,1,0:T(8,128)(2,1)S(1)}, u32[]{:S(2)}, u32[]{:S(2)}) collective-permute-start(bf16[16,96,256]{2,1,0:T(8,128)(2,1)S(1)} %all-to-all-done.c_ref.own_s), channel_id=1, source_target_pairs={{0,32},{32,0},{1,33},{33,1},{2,34},{34,2},{3,35},{35,3},{4,36},{36... | collective-permute-start | bytes 2359304 | tf_op jit(solution)/shard_map/ppermute | solution.py:285
  31.2 6.9 %first_half.1 = (f32[16,2048]{1,0:T(8,128)S(1)}, bf16[80,2048]{1,0:T(8,128)(2,1)S(1)}, bf16[512,2048]{1,0:T(8,128)(2,1)S(1)}, bf16[512,2048]{1,0:T(8,128)(2,1)S(...) custom-call(bf16[16,96,256]{2,1,0:T(8,128)(2,1)S(1)} %all-to-all-don, ...), custom_call_target="tpu_custom_call" | custom-call | tf_op jit(solution)/shard_map/first_half/pallas_call | solution.py:322
  38.1 0.0 collective-permute-done.4.c_ref.other_s
  38.1 7.1 %second_half.1 = (f32[8,16,256]{2,1,0:T(8,128)S(1)}, bf16[512,2048]{1,0:T(8,128)(2,1)S(1)}, bf16[512,2048]{1,0:T(8,128)(2,1)S(1)}, bf16[512,2048]{1,0:T(8,128)(2...) custom-call(s32[1]{0:T(128)} %bitcast.place, ...), custom_call_target="tpu_custom_call" | custom-call | tf_op jit(solution)/shard_map/second_half/pallas_call | solution.py:331
  45.3 11.6 %all_to_all.30.parts = f32[8,16,256]{2,1,0:T(8,128)S(1)} all-to-all(f32[8,16,256]{2,1,0:T(8,128)S(1)} %get-tuple-element.48), channel_id=1, replica_groups=mesh['y'=4,'core'=2,'z'=8,'x'=4] {'z'}, dimensions={0} | all-to-all | bytes 262144 | tf_op jit(solution)/shard_map/all_to_all | solution.py:341
  56.9 0.0 copy-done
  56.9 0.0 copy-done.2
  56.9 0.2 first_image.1
  57.1 14.7 %all_to_all.31.own.own_i = f32[16,24,256]{2,1,0:T(8,128)S(1)} all-to-all(f32[16,24,256]{2,1,0:T(8,128)S(1)} %get-tuple-element.51), channel_id=1, replica_groups=mesh['y'=4,'core'=2,'z'=8,'x'=4] {'y','x'}, dimensions={0} | all-to-all | bytes 786432 | tf_op jit(solution)/shard_map/all_to_all | solution.py:348
  71.8 2.9 %collective-permute-start.5 = (f32[16,24,256]{2,1,0:T(8,128)S(1)}, f32[16,24,256]{2,1,0:T(8,128)S(1)}, u32[]{:S(2)}, u32[]{:S(2)}) collective-permute-start(f32[16,24,256]{2,1,0:T(8,128)S(1)} %all_to_all.31.own.own_i), channel_id=1, source_target_pairs={{0,32},{32,0},{1,33},{33,1},{2,34},{34,2},{3,35},{35,3},{4,36},{36... | collective-permute-start | bytes 1179656 | tf_op jit(solution)/shard_map/ppermute | solution.py:285
  74.8 1.3 %collective-permute-done.5.other.other_i = f32[16,24,256]{2,1,0:T(8,128)S(1)} collective-permute-done((f32[16,24,256]{2,1,0:T(8,128)S(1)}, f32[16,24,256]{2,1,0:T(8,128)S(1)}, u32[]{:S(2)}, u32[]{:S(2)}) %collective-permute-start.5) | collective-permute-done | bytes 393248 | tf_op jit(solution)/shard_map/ppermute | solution.py:285
  76.1 12.5 %all_to_all.32.along_z = bf16[8,48,256]{2,1,0:T(8,128)(2,1)S(1)} all-to-all(bf16[8,48,256]{2,1,0:T(8,128)(2,1)S(1)} %gram_sum.1), channel_id=1, replica_groups=mesh['y'=4,'core'=2,'z'=8,'x'=4] {'z'}, dimensions={0} | all-to-all | bytes 393216 | tf_op jit(solution)/shard_map/all_to_all | solution.py:360
  88.6 6.9 %second_apply.1 = (f32[8,24,256]{2,1,0:T(8,128)S(1)}, f32[16,256]{1,0:T(8,128)S(1)}, f32[16,256]{1,0:T(8,128)S(1)}, f32[16,256]{1,0:T(8,128)S(1)}, f32[16,16]{1,0:T(8,128)S(1)}) custom-call(s32[1]{0:T(128)} %bitcast.place, bf16[8,48,256]{2,1,0:T(8,128)(2,1)S(1)} %all_to_all.32.along_z, f32[16,24,256]{2,1,0:T(8,128)S(1)} %all_to_all.31.own.own_i, ...), custom_call_target="tpu_custom_call" | custom-call | tf_op jit(solution)/shard_map/second_apply/pallas_call | solution.py:364
  95.5 10.8 %all_to_all.33.parts = f32[8,24,256]{2,1,0:T(8,128)S(1)} all-to-all(f32[8,24,256]{2,1,0:T(8,128)S(1)} %get-tuple-element.71), channel_id=1, replica_groups=mesh['y'=4,'core'=2,'z'=8,'x'=4] {'z'}, dimensions={0} | all-to-all | bytes 393216 | tf_op jit(solution)/shard_map/all_to_all | solution.py:380
  106.3 0.2 second_image.1
  106.5 13.2 %all_to_all.34.grams = f32[32,2,128]{2,1,0:T(2,128)S(1)} all-to-all(f32[32,2,128]{2,1,0:T(2,128)S(1)} %get-tuple-element.73), channel_id=1, replica_groups=mesh['y'=4,'core'=2,'z'=8,'x'=4] {'y','core','x'}, dimensions={0} | all-to-all | bytes 65536 | tf_op jit(solution)/shard_map/all_to_all | solution.py:385
  119.7 1.3 %finish.1 = (f32[16,256]{1,0:T(8,128)}, f32[16,256]{1,0:T(8,128)}) custom-call(f32[32,2,128]{2,1,0:T(2,128)S(1)} %all_to_all.34.grams, f32[16,16]{1,0:T(8,128)S(1)} %get-tuple-element.74.gram1, f32[16,256]{1,0:T(8,128)S(1)} %get-tuple-element.75.sol1, f32[16,256]{1,0:T(8,128)S(1)} %get-tuple-element.76.res1, f32[16,256]{1,0:T(8,128)S(1)} %get-tuple-element.72.base.dir1, ...), custom_call_target="tpu_custom_call" | custom-call | tf_op jit(solution)/shard_map/finish/pallas_call | solution.py:386
  (3 shorter events, 0.0 us)
Async XLA Ops:
  3.2 53.6 %copy-start = (f32[16,256]{1,0:T(8,128)S(1)}, f32[16,256]{1,0:T(8,128)}, u32[]{:S(2)}) copy-start(f32[16,256]{1,0:T(8,128)} %get-tuple-element.49.base.more_0_) | copy-start | bytes 49156
  3.3 53.6 %copy-start.2 = (f32[1,256]{1,0:T(1,128)S(1)}, f32[1,256]{1,0:T(1,128)}, u32[]{:S(2)}) copy-start(f32[1,256]{1,0:T(1,128)} %get-tuple-element.50.w) | copy-start | bytes 3076
  3.3 24.1 %all-to-all-start = ((bf16[16,96,256]{2,1,0:T(8,128)(2,1)}), bf16[16,96,256]{2,1,0:T(8,128)(2,1)S(1)}, u32[]{:S(2)}, u32[]{:S(2)}) async-start(bf16[16,96,256]{2,1,0:T(8,128)(2,1)} %get-tuple-element.40), calls=%async_computation | async-start | bytes 1572864 | tf_op jit(solution)/shard_map/all_to_all | solution.py:311
  10.9 65.2 %copy-start.1 = (bf16[16,256]{1,0:T(8,128)(2,1)S(1)}, bf16[16,256]{1,0:T(8,128)(2,1)}, u32[]{:S(2)}) copy-start(bf16[16,256]{1,0:T(8,128)(2,1)} %get-tuple-element.52.scaled) | copy-start | bytes 24580
  10.9 3.2 %collective-permute-start = (bf16[64,256]{1,0:T(8,128)(2,1)}, bf16[64,256]{1,0:T(8,128)(2,1)S(1)}, u32[]{:S(2)}, u32[]{:S(2)}) collective-permute-start(bf16[64,256]{1,0:T(8,128)(2,1)} %emb_in.1), channel_id=1, source_target_pairs={{0,4},{4,0},{8,12},{12,8},{16,20},{20,16},{24,28},{28,24},{1,5},{5... | collective-permute-start | bytes 98312 | tf_op jit(solution)/shard_map/ppermute | solution.py:281
  14.1 8.7 %collective-permute-start.3 = (bf16[64,512]{1,0:T(8,128)(2,1)S(1)}, bf16[64,512]{1,0:T(8,128)(2,1)S(1)}, u32[]{:S(2)}, u32[]{:S(2)}) collective-permute-start(bf16[64,512]{1,0:T(8,128)(2,1)S(1)} %constant_dynamic-update-slice_fusion.more_0_), channel_id=1, source_target_pairs={{0,16},{4,20},{8,24},{12,28},{16,0},{20,4},{24,8},{28,12},{1,17},{... | collective-permute-start | bytes 196616 | tf_op jit(solution)/shard_map/ppermute | solution.py:281
  20.9 6.2 %collective-permute-start.2 = (bf16[64,512]{1,0:T(8,128)(2,1)S(1)}, bf16[64,512]{1,0:T(8,128)(2,1)S(1)}, u32[]{:S(2)}, u32[]{:S(2)}) collective-permute-start(bf16[64,512]{1,0:T(8,128)(2,1)S(1)} %constant_dynamic-update-slice_fusion.more_0_), channel_id=1, source_target_pairs={{0,8},{4,12},{8,0},{12,4},{16,24},{20,28},{24,16},{28,20},{1,9},{5... | collective-permute-start | bytes 196616 | tf_op jit(solution)/shard_map/ppermute | solution.py:281
  22.1 5.3 %collective-permute-start.1 = (bf16[64,512]{1,0:T(8,128)(2,1)S(1)}, bf16[64,512]{1,0:T(8,128)(2,1)S(1)}, u32[]{:S(2)}, u32[]{:S(2)}) collective-permute-start(bf16[64,512]{1,0:T(8,128)(2,1)S(1)} %constant_dynamic-update-slice_fusion.more_0_), channel_id=1, source_target_pairs={{0,24},{4,28},{8,16},{12,20},{16,8},{20,12},{24,0},{28,4},{1,25},{... | collective-permute-start | bytes 196616 | tf_op jit(solution)/shard_map/ppermute | solution.py:281
  27.4 10.7 %collective-permute-start.4 = (bf16[16,96,256]{2,1,0:T(8,128)(2,1)S(1)}, bf16[16,96,256]{2,1,0:T(8,128)(2,1)S(1)}, u32[]{:S(2)}, u32[]{:S(2)}) collective-permute-start(bf16[16,96,256]{2,1,0:T(8,128)(2,1)S(1)} %all-to-all-done.c_ref.own_s), channel_id=1, source_target_pairs={{0,32},{32,0},{1,33},{33,1},{2,34},{34,2},{3,35},{35,3},{4,36},{36... | collective-permute-start | bytes 2359304 | tf_op jit(solution)/shard_map/ppermute | solution.py:285
  71.8 4.3 %collective-permute-start.5 = (f32[16,24,256]{2,1,0:T(8,128)S(1)}, f32[16,24,256]{2,1,0:T(8,128)S(1)}, u32[]{:S(2)}, u32[]{:S(2)}) collective-permute-start(f32[16,24,256]{2,1,0:T(8,128)S(1)} %all_to_all.31.own.own_i), channel_id=1, source_target_pairs={{0,32},{32,0},{1,33},{33,1},{2,34},{34,2},{3,35},{35,3},{4,36},{36... | collective-permute-start | bytes 1179656 | tf_op jit(solution)/shard_map/ppermute | solution.py:285
